TPU v7x, 512 devices: a whole 4x8x8 slice. The times are simulated.
512 devices in a mesh: wide: 64 (over z, x, y_lo), narrow: 8 (over y_hi, core).
Axes of the slice: x: 4, y: 8 (y_hi: 4, y_lo: 2; y = y_hi * 2 + y_lo), z: 8, core: 2. Of those that a mesh axis runs over, the one named last changes fastest.
Arguments:
- output_gradient: bfloat16 [1024, 16384], P('wide', 'narrow'), may hold values from -6 to 6
- packed_weight_codes: int32 [49152, 8192], P('wide', 'narrow'), may hold values from 0 to 255
- group_zero_offsets: int32 [384, 16384], P('wide', 'narrow'), may hold values from 0 to 15
- group_scale_table: float32 [384, 16384], P('wide', 'narrow'), may hold values from 0.0004 to 0.004
- channel_aware_scale: float32 [49152], P('wide'), may hold values from 0.5 to 2
- adapter_down_matrix: bfloat16 [49152, 16], P('wide'), may hold values from -1.5 to 1.5
- adapter_up_matrix: bfloat16 [16, 16384], P(None, 'narrow'), may hold values from -0.046875 to 0.046875
Outputs:
- grad_input: bfloat16 [1024, 49152], P('narrow', 'wide')
Inputs may be any that keep to these rules, and one draw needn't show every extreme that they name: `packed_weight_codes`: word column 128 * b + i holds the code of output column 2 * 128 * b + i in its value modulo 16 and that of column 2 * 128 * b + 128 + i in its value divided by 16.
All inputs are finite; a program needn't handle non-finite values.
Results may differ from a plain program's by a relative error of at most 0.0048.
Values may be sent and summed in bfloat16 or wider, within the bound.
No kernel may reach another device: no remote copies, remote signals or barrier semaphores. Data moves between devices by JAX's collectives and lax.ppermute only.
A program may use at most 128 MiB of HBM per device.

v0:
```python
import jax
import jax.numpy as jnp
from jax import lax
from jax.sharding import PartitionSpec as P

GROUP = 128
HALF = 128


adapter_gain = 0.5


def unpack(words, zero_rows, scale_rows):
    rows, half_cols = words.shape
    low_codes = words % 16
    high_codes = words // 16
    blocks = half_cols // HALF
    codes = jnp.stack(
        [low_codes.reshape(rows, blocks, HALF), high_codes.reshape(rows, blocks, HALF)], axis=2
    ).reshape(rows, 2 * half_cols)
    groups = rows // GROUP
    shifted = (codes.reshape(groups, GROUP, 2 * half_cols) - zero_rows[:, None, :]).astype(
        jnp.float32
    )
    return (shifted * scale_rows[:, None, :]).reshape(rows, 2 * half_cols).astype(jnp.bfloat16)


def shards(
    output_gradient,
    packed_weight_codes,
    group_zero_offsets,
    group_scale_table,
    channel_aware_scale,
    adapter_down_matrix,
    adapter_up_matrix,
):
    weight = unpack(packed_weight_codes, group_zero_offsets, group_scale_table)
    dequantized_down = adapter_down_matrix.astype(jnp.float32)
    collected_rows = lax.all_gather(output_gradient, "wide", axis=0, tiled=True)
    adapter_inner_piece = jnp.einsum(
        "ch,jh->cj", collected_rows, adapter_up_matrix, preferred_element_type=jnp.float32
    )
    total = collected_rows.shape[0]
    own_count = total // lax.axis_size("narrow")
    adapter_inner_total = lax.psum(adapter_inner_piece, "narrow")
    local_owned_rows = lax.psum_scatter(
        jnp.einsum("td,kd->tk", collected_rows, weight, preferred_element_type=jnp.float32)
        / channel_aware_scale[None, :],
        "narrow",
        scatter_dimension=0,
        tiled=True,
    )
    own_start = lax.axis_index("narrow") * own_count
    own_inner = lax.dynamic_slice_in_dim(adapter_inner_total, own_start, own_count, 0)
    local_owned_rows = local_owned_rows + adapter_gain * jnp.dot(
        own_inner, dequantized_down.T, precision=lax.Precision.HIGHEST
    )
    return local_owned_rows.astype(jnp.bfloat16)


def solution(mesh):
    placed = (
        P("wide", "narrow"),
        P("wide", "narrow"),
        P("wide", "narrow"),
        P("wide", "narrow"),
        P("wide"),
        P("wide", None),
        P(None, "narrow"),
    )
    return jax.shard_map(
        shards, mesh=mesh, in_specs=placed, out_specs=P("narrow", "wide"), check_vma=False
    )
```

profile of v0, /device:TPU:70, one launch (start us, length us, event | category | flops | bytes accessed | tf_op | source)
XLA Modules:
  0.0 467.5 jit_solution(12338306852317907402)
XLA Ops:
  6.5 0.0 copy-start
  6.5 0.0 all-gather.2.cloned.1.call-start
  6.5 0.7 all-gather.2.cloned.1.call-update
  7.3 0.0 all-reduce.2.cloned.1.call-start
  7.3 4.3 mul.20
  11.6 0.0 copy-start.2
  11.6 6.6 %copy.19 = f32[768,2048]{0,1:T(8,128)} copy(f32[768,2048]{1,0:T(8,128)} %bitcast.19) | data formatting | bytes 12582912 | tf_op jit(solution)/shard_map/mul | solution.py:25
  18.2 0.0 copy-done.2
  18.2 3.4 sub.18
  21.5 6.6 %copy.18 = s32[768,2048]{0,1:T(8,128)} copy(s32[768,2048]{1,0:T(8,128)} %bitcast.20) | data formatting | bytes 12582912 | tf_op jit(solution)/shard_map/sub | solution.py:22
  28.1 6.2 %add_select_fusion.1 = (s32[768,1024]{1,0:T(8,128)S(1)}, s32[768,1024]{1,0:T(8,128)}) fusion(s32[768,1024]{1,0:T(8,128)} %param.8), kind=kLoop, calls=%fused_computation.7 | loop fusion | flops 14942208 | bytes 9437184 | tf_op jit(solution)/shard_map/jit(remainder)/select_n | solution.py:15
  34.2 3.6 copy.17
  37.9 2.4 copy.16
  40.2 0.0 slice-start
  40.2 0.0 slice-start.1
  40.2 6.2 %pad_add_fusion = s32[768,8,2,128]{0,3,2,1:T(8,128)} fusion(s32[768,8,1,128]{0,3,2,1:T(8,128)} %bitcast.23, s32[768,8,1,128]{0,3,2,1:T(8,128)} %bitcast.24), kind=kLoop, calls=%fused_computation | loop fusion | flops 1572864 | bytes 12582912 | tf_op jit(solution)/shard_map/stack | solution.py:18
  46.4 0.0 slice-done
  46.4 0.0 slice-done.1
  46.4 8.1 %fusion.2 = bf16[768,2048]{0,1:T(8,128)(2,1)} fusion(f32[768,2048]{0,1:T(8,128)S(1)} %bitcast.22, s32[768,2048]{0,1:T(8,128)} %copy.18, s32[768,8,2,128]{0,3,2,1:T(8,128)} %pad_add_fusion), kind=kLoop, calls=%fused_computation.4 | loop fusion | flops 6291456 | bytes 22020096 | tf_op jit(solution)/shard_map/convert_element_type | solution.py:25
  54.6 0.0 copy-start.1
  54.6 0.0 copy-start.4
  54.6 249.0 %all-gather.2.cloned.1.call-done = bf16[1024,2048]{1,0:T(8,128)(2,1)} async-done(((bf16[16,2048]{1,0:T(8,128)(2,1)}), bf16[1024,2048]{1,0:T(8,128)(2,1)}) %all-gather.2.cloned.1.call-update) | async-done | bytes 4194320 | tf_op jit(solution)/shard_map/all_gather | solution.py:39
  303.6 0.0 copy-done
  303.6 4.0 fusion.9
  307.6 0.0 all-reduce.2.cloned.1.call-update
  307.6 0.2 reduce-scatter.2.cloned.1.call-start
  307.9 0.0 copy-done.1
  307.9 0.0 copy-done.4
  307.9 7.4 %divide_bitcast_fusion = f32[1024,768]{0,1:T(8,128)} fusion(bf16[768,2048]{0,1:T(8,128)(2,1)S(1)} %copy-done.1, bf16[1024,2048]{1,0:T(8,128)(2,1)} %all-gather.2.cloned.1.call-done, f32[768]{0:T(1024)S(1)} %copy-done.4), kind=kOutput, calls=%fused_computation.10 | convolution fusion | flops 3222011904 | bytes 10488832 | tf_op jit(solution)/shard_map/td,kd->tk/dot_general | solution.py:47
  315.3 0.0 copy-start.3
  315.3 0.0 reduce-scatter.2.cloned.1.call-update
  315.3 87.6 %all-reduce.2.cloned.1.call-done = f32[1024,16]{0,1:T(8,128)} async-done(((f32[1024,16]{0,1:T(8,128)}), f32[1024,16]{0,1:T(8,128)}) %all-reduce.2.cloned.1.call-update) | async-done | bytes 65552 | tf_op jit(solution)/shard_map/psum | solution.py:45
  402.9 55.9 %reduce-scatter.2.cloned.1.call-done = f32[128,768]{0,1:T(8,128)} async-done(((f32[1024,768]{0,1:T(8,128)}), f32[128,768]{0,1:T(8,128)}) %reduce-scatter.2.cloned.1.call-update) | async-done | bytes 393232 | tf_op jit(solution)/shard_map/reduce_scatter | solution.py:46
  458.7 0.0 copy-done.3
  458.7 1.4 fusion.6
  460.1 0.8 copy.21
  (1 shorter events, 0.0 us)
Async XLA Ops:
  6.5 297.1 %copy-start = (bf16[16,2048]{1,0:T(8,128)(2,1)S(1)}, bf16[16,2048]{1,0:T(8,128)(2,1)}, u32[]{:S(2)}) copy-start(bf16[16,2048]{1,0:T(8,128)(2,1)} %param.13) | copy-start | bytes 196612
  6.5 297.1 %all-gather.2.cloned.1.call-start = ((), (), s32[]{:S(2)}) async-start(), calls=%async_computation.1 | async-start | bytes 4259840 | tf_op jit(solution)/shard_map/all_gather | solution.py:39
  7.3 395.6 %all-reduce.2.cloned.1.call-start = ((), (), s32[]{:S(2)}) async-start(), calls=%async_computation.3 | async-start | bytes 131072 | tf_op jit(solution)/shard_map/psum | solution.py:45
  11.6 6.6 %copy-start.2 = (s32[6,2048]{1,0:T(8,128)S(1)}, s32[6,2048]{1,0:T(8,128)}, u32[]{:S(2)}) copy-start(s32[6,2048]{1,0:T(8,128)} %param.9) | copy-start | bytes 147460
  40.2 6.2 %slice-start = ((s8[6291456]{0:T(1024)(128)(4,1)}), s8[4194304]{0:T(1024)(128)(4,1)S(1)}, s32[]{:S(2)}) async-start(s8[6291456]{0:T(1024)(128)(4,1)} %bitcast.21), calls=%async_computation.4 | async-start | bytes 8388608
  40.2 6.2 %slice-start.1 = ((s8[6291456]{0:T(1024)(128)(4,1)}), s8[2097152]{0:T(1024)(128)(4,1)S(1)}, s32[]{:S(2)}) async-start(s8[6291456]{0:T(1024)(128)(4,1)} %bitcast.21), calls=%async_computation.5 | async-start | bytes 4194304
  54.6 253.3 %copy-start.1 = (bf16[768,2048]{0,1:T(8,128)(2,1)S(1)}, bf16[768,2048]{0,1:T(8,128)(2,1)}, u32[]{:S(2)}) copy-start(bf16[768,2048]{0,1:T(8,128)(2,1)} %fusion.2) | copy-start | bytes 9437188
  54.6 253.3 %copy-start.4 = (f32[768]{0:T(1024)S(1)}, f32[768]{0:T(1024)}, u32[]{:S(2)}) copy-start(f32[768]{0:T(1024)} %param.11) | copy-start | bytes 9220
  307.6 151.1 %reduce-scatter.2.cloned.1.call-start = ((), (), s32[]{:S(2)}) async-start(), calls=%async_computation.2 | async-start | bytes 3538944 | tf_op jit(solution)/shard_map/reduce_scatter | solution.py:46
  315.3 143.5 %copy-start.3 = (bf16[768,16]{0,1:T(8,128)(2,1)S(1)}, bf16[768,16]{0,1:T(8,128)(2,1)}, u32[]{:S(2)}) copy-start(bf16[768,16]{0,1:T(8,128)(2,1)} %param.12) | copy-start | bytes 73732
Sparse Core Ops, SparseCore 0:
  9.4 294.1 all-gather.1
  307.8 95.0 all-reduce.1
  406.0 52.7 reduce-scatter.1
where the time goes:
time: 468 us; the launch traced here: 467 us
  waiting for transfers between devices  393 us (84%)
  local copies, waits for them, and re-layouts  27.6 us (6%)
  other arithmetic  20.5 us (4%)
  between operations  13.1 us (3%)
  matrix products  12.8 us (3%)
    all_gather x1, waiting for transfers between devices, shards(): collected_rows = lax.all_gather(output_gradient, 'wide', axis=0, tiled=True)  249 us
    psum x1, waiting for transfers between devices, shards(): adapter_inner_total = lax.psum(adapter_inner_piece, 'narrow')  87.6 us
    reduce_scatter x1, waiting for transfers between devices, shards(): lax.psum_scatter(jnp.einsum('td,kd->tk', collected_rows, weight, preferre...  55.9 us
    mul x2, local copies, waits for them, and re-layouts, unpack(): shifted * scale_rows[:, None, :]  10.9 us
    sub x2, local copies, waits for them, and re-layouts, unpack(): codes.reshape(groups, GROUP, 2 * half_cols) - zero_rows[:, None, :]  9.91 us
  transfers between devices with their start and end apart: 3, of which 3 were waited for; matrix products, arithmetic and copies ran while one was open for 12% of the time, Pallas kernels for 0%

commit v1 on v0

v1 whole, which is shorter than its diff:
```python
import jax
import jax.numpy as jnp
from jax import lax
from jax.experimental import pallas as pl
from jax.experimental.pallas import tpu as pltpu
from jax.sharding import PartitionSpec as P

GROUP = 128
HALF = 128
ADAPTER_GAIN = 0.5

Z, X, YLO, YHI, CORE = 8, 4, 2, 4, 2
PLANE = X * YLO

PLANES = [[z * PLANE + p for p in range(PLANE)] for z in range(Z)]
OTHER_CORE = [(h * CORE + c, h * CORE + 1 - c) for h in range(YHI) for c in range(CORE)]


BOTH = ("wide", "narrow")


def device(z, place, h, core):
    return ((z % Z * PLANE + place) * YHI + h) * CORE + core


SPOTS = [(z, place, h) for z in range(Z) for place in range(PLANE) for h in range(YHI)]
TO_HOME = [(device(z, p, h, 1 - z % 2), device(z, p, h, z % 2)) for z, p, h in SPOTS]

OWNERS = [
    [device(z, p, ((z + (c != z % 2)) % Z // 2 + j) % YHI, c) for j in range(YHI)]
    for z in range(Z)
    for p in range(PLANE)
    for c in range(CORE)
]


def hop(step, from_home):
    cores = [(z, p, h, z % 2 if from_home else 1 - z % 2) for z, p, h in SPOTS]
    return [(device(z, p, h, c), device(z + step, p, h, c)) for z, p, h, c in cores]


def pick_row(table, index):
    rows = lax.broadcasted_iota(jnp.int32, table.shape, 0)
    return jnp.sum(jnp.where(rows == index, table, 0), axis=0, keepdims=True)


def pick_row(table, index):
    rows = lax.broadcasted_iota(jnp.int32, table.shape, 0)
    return jnp.sum(jnp.where(rows == index, table, 0), axis=0, keepdims=True)


def weight_kernel(words_ref, zero_ref, scale_ref, channel_ref, down_ref, up_ref, out_ref):
    group = pl.program_id(0)
    square = (GROUP, GROUP)
    diagonal = lax.broadcasted_iota(jnp.int32, square, 0) == lax.broadcasted_iota(jnp.int32, square, 1)
    channel = jnp.sum(jnp.where(diagonal, channel_ref[...], 0.0), axis=1, keepdims=True)
    inverse = 1.0 / channel
    down = down_ref[...]
    for block in range(words_ref.shape[1] // HALF):
        words = words_ref[:, block * HALF : (block + 1) * HALF]
        for half, codes in enumerate((words & 15, words >> 4)):
            columns = pl.ds((2 * block + half) * HALF, HALF)
            zero = pick_row(zero_ref[:, columns], group)
            scale = pick_row(scale_ref[:, columns], group)
            weight = ((codes - zero).astype(jnp.float32) * scale).astype(jnp.bfloat16)
            adapter = lax.dot_general(
                down, up_ref[:, columns], (((0,), (0,)), ((), ())), preferred_element_type=jnp.float32
            )
            out_ref[:, columns] = (
                weight.astype(jnp.float32) * inverse + ADAPTER_GAIN * adapter
            ).astype(jnp.bfloat16)


def effective_weight(words, zeros, scales, channel, down, up):
    rows, half_cols = words.shape
    cols = 2 * half_cols
    groups = rows // GROUP
    rank = down.shape[1]
    return pl.pallas_call(
        weight_kernel,
        grid=(groups,),
        in_specs=[
            pl.BlockSpec((GROUP, half_cols), lambda g: (g, 0)),
            pl.BlockSpec((groups, cols), lambda g: (0, 0)),
            pl.BlockSpec((groups, cols), lambda g: (0, 0)),
            pl.BlockSpec((1, GROUP), lambda g: (0, g)),
            pl.BlockSpec((rank, GROUP), lambda g: (0, g)),
            pl.BlockSpec((rank, cols), lambda g: (0, 0)),
        ],
        out_specs=pl.BlockSpec((GROUP, cols), lambda g: (g, 0)),
        out_shape=jax.ShapeDtypeStruct((rows, cols), jnp.bfloat16),
        compiler_params=pltpu.CompilerParams(vmem_limit_bytes=8 * 1024 * 1024),
        cost_estimate=pl.CostEstimate(
            flops=12 * rows * cols, bytes_accessed=4 * rows * half_cols + 2 * rows * cols, transcendentals=0
        ),
    )(words, zeros, scales, channel.reshape(1, rows), down.T, up)


def send_all(block, groups):
    copies = jnp.broadcast_to(block[None], (len(groups[0]),) + block.shape)
    return lax.all_to_all(copies, "wide", 0, 0, axis_index_groups=groups)


def times(block, weight, other_weight):
    dims = (((1,), (1,)), ((), ()))
    return lax.dot_general(block[0], weight, dims, preferred_element_type=jnp.float32) + lax.dot_general(
        block[1], other_weight, dims, preferred_element_type=jnp.float32
    )


def shards(grad, words, zeros, scales, channel, down, up):
    rows, cols = grad.shape
    k = words.shape[0]
    tokens = PLANE * rows
    mid = tokens // 2
    z = lax.axis_index("wide") >> 3
    core = lax.axis_index("narrow") & 1
    home = core == (z & 1)

    own = send_all(grad, PLANES).reshape(tokens, cols)
    own = jnp.stack([own, lax.ppermute(own, BOTH, TO_HOME)])

    weight = effective_weight(words, zeros, scales, channel + 0 * own[1, 0, :k].astype(jnp.float32), down, up)
    other_weight = jnp.concatenate(
        [lax.ppermute(weight[i : i + 256], "narrow", OTHER_CORE) for i in range(0, k, 256)], 0
    )
    low, high = [own], [own]
    for step in range(3):
        low.append(lax.ppermute(low[-1], BOTH, hop(1, step % 2 == 0)))
        high.append(lax.ppermute(high[-1], BOTH, hop(-1, step % 2 == 0)))
    far = jnp.concatenate(
        [
            lax.ppermute(low[3][:, :mid], BOTH, hop(1, False)),
            lax.ppermute(high[3][:, mid:], BOTH, hop(-1, False)),
        ],
        1,
    )
    blocks = [
        jnp.where(home, own, high[1]),
        jnp.where(home, high[2], high[3]),
        jnp.where(home, far, low[3]),
        jnp.where(home, low[2], low[1]),
    ]
    blocks = [lax.optimization_barrier(block) for block in blocks]
    parts = jnp.stack([times(block, weight, other_weight).astype(jnp.bfloat16) for block in blocks])
    parts = lax.all_to_all(parts, BOTH, 0, 0, axis_index_groups=OWNERS)
    return jnp.sum(parts.astype(jnp.float32), axis=0).astype(jnp.bfloat16)


def solution(mesh):
    placed = (
        P("wide", "narrow"),
        P("wide", "narrow"),
        P("wide", "narrow"),
        P("wide", "narrow"),
        P("wide"),
        P("wide", None),
        P(None, "narrow"),
    )
    return jax.shard_map(
        shards, mesh=mesh, in_specs=placed, out_specs=P("narrow", "wide"), check_vma=False
    )
```

time: 468 us -> 122 us (0.26)
  the two profiles are of different devices: /device:TPU:70 before, /device:TPU:64 now
where the time goes in v1:
time: 122 us; the launch traced here: 121 us
  blocking collectives  41.9 us (34%)
  starting transfers between devices  27.9 us (23%)
  waiting for transfers between devices  26.3 us (22%)
  matrix products  9.4 us (8%)
  local copies, waits for them, and re-layouts  6.83 us (6%)
  other arithmetic  5.63 us (5%)
  Pallas kernels  3.02 us (2%)
    all_to_all x1, blocking collectives, shards(): parts = lax.all_to_all(parts, BOTH, 0, 0, axis_index_groups=OWNERS)  26.6 us
    all_to_all x1, blocking collectives, send_all(): return lax.all_to_all(copies, 'wide', 0, 0, axis_index_groups=groups)  15.2 us
    ppermute x3, waiting for transfers between devices, shards(): high.append(lax.ppermute(high[-1], BOTH, hop(-1, step % 2 == 0)))  14.3 us
    ppermute x3, starting transfers between devices, shards(): lax.ppermute(weight[i:i + 256], 'narrow', OTHER_CORE)  12 us
    ppermute x3, starting transfers between devices, shards(): high.append(lax.ppermute(high[-1], BOTH, hop(-1, step % 2 == 0)))  6.76 us
    ppermute x3, waiting for transfers between devices, shards(): low.append(lax.ppermute(low[-1], BOTH, hop(1, step % 2 == 0)))  6.26 us
    dot_general x4, matrix products, times(): lax.dot_general(block[1], other_weight, dims, preferred_element_type=jnp....  4.7 us
    dot_general x4, matrix products, times(): lax.dot_general(block[0], weight, dims, preferred_element_type=jnp.float32)  4.7 us
  transfers between devices with their start and end apart: 12, of which 6 were waited for; matrix products, arithmetic and copies ran while one was open for 13% of the time, Pallas kernels for 2%

profile of v1, /device:TPU:64, one launch (start us, length us, event | category | flops | bytes accessed | tf_op | source)
XLA Modules:
  0.0 121.3 jit_solution(14956933123911642820)
XLA Ops:
  0.0 0.0 copy-start.7
  0.0 0.0 copy-start
  0.0 0.0 copy-start.1
  0.0 0.0 copy-start.2
  0.0 0.0 copy-start.4
  0.0 0.0 copy-start.3
  0.0 1.0 broadcast_in_dim.2
  1.1 15.2 %all_to_all.10 = bf16[8,16,2048]{2,1,0:T(8,128)(2,1)S(1)} all-to-all(bf16[8,16,2048]{2,1,0:T(8,128)(2,1)S(1)} %broadcast_in_dim.2), channel_id=1, replica_groups={{0,8,16,24,32,40,48,56},{64,72,80,88,96,104,112,120},{128,136,144,152,1..., dimensions={0} | all-to-all | bytes 1048576 | tf_op jit(solution)/shard_map/all_to_all | solution.py:101
  16.3 0.0 copy-start.5
  16.3 1.3 %collective-permute-start = (bf16[128,2048]{1,0:T(8,128)(2,1)S(1)}, bf16[128,2048]{1,0:T(8,128)(2,1)S(1)}, u32[]{:S(2)}, u32[]{:S(2)}) collective-permute-start(bf16[128,2048]{1,0:T(8,128)(2,1)S(1)} %bitcast.45), channel_id=1, source_target_pairs={{1,0},{3,2},{5,4},{7,6},{9,8},{11,10},{13,12},{15,14},{17,16},{19,... | collective-permute-start | bytes 1572872 | tf_op jit(solution)/shard_map/ppermute | solution.py:121
  17.6 1.5 %collective-permute-done = bf16[128,2048]{1,0:T(8,128)(2,1)S(1)} collective-permute-done((bf16[128,2048]{1,0:T(8,128)(2,1)S(1)}, bf16[128,2048]{1,0:T(8,128)(2,1)S(1)}, u32[]{:S(2)}, u32[]{:S(2)}) %collective-permute-start) | collective-permute-done | bytes 524320 | tf_op jit(solution)/shard_map/ppermute | solution.py:121
  19.1 0.0 copy-start.6
  19.1 1.2 pad_maximum_fusion
  20.3 1.3 %collective-permute-start.7 = (bf16[2,128,2048]{2,1,0:T(8,128)(2,1)}, bf16[2,128,2048]{2,1,0:T(8,128)(2,1)}, u32[]{:S(2)}, u32[]{:S(2)}) collective-permute-start(bf16[2,128,2048]{2,1,0:T(8,128)(2,1)} %pad_maximum_fusion), channel_id=1, source_target_pairs={{0,64},{2,66},{4,68},{6,70},{8,72},{10,74},{12,76},{14,78},{16,80}... | collective-permute-start | bytes 3145736 | tf_op jit(solution)/shard_map/ppermute | solution.py:129
  21.6 1.3 %collective-permute-start.1 = (bf16[2,128,2048]{2,1,0:T(8,128)(2,1)}, bf16[2,128,2048]{2,1,0:T(8,128)(2,1)}, u32[]{:S(2)}, u32[]{:S(2)}) collective-permute-start(bf16[2,128,2048]{2,1,0:T(8,128)(2,1)} %pad_maximum_fusion), channel_id=1, source_target_pairs={{0,448},{2,450},{4,452},{6,454},{8,456},{10,458},{12,460},{14,462}... | collective-permute-start | bytes 3145736 | tf_op jit(solution)/shard_map/ppermute | solution.py:130
  22.9 0.0 copy-done.7
  22.9 0.0 copy-done.5
  22.9 0.0 copy-done.6
  22.9 0.0 copy-done
  22.9 0.0 copy-done.1
  23.0 0.0 copy-done.2
  23.0 0.0 copy-done.4
  23.0 0.0 copy-done.3
  23.0 3.0 %shard_map.73 = bf16[768,2048]{1,0:T(8,128)(2,1)S(1)} custom-call(s32[768,1024]{1,0:T(8,128)S(1)} %copy-done, s32[6,2048]{1,0:T(8,128)S(1)} %copy-done.1, f32[6,2048]{1,0:T(8,128)S(1)} %copy-done.2, f32[1,768]{1,0:T(1,128)S(1)} %reshape.11.channel_ref, bf16[16,768]{1,0:T(8,128)(2,1)S(1)} %bitcast.44, bf16[16,2048]{1,0:T(8,128)(2,1)S(1)} %copy-done.3), custom_call_target="tpu_custom_call" | custom-call | flops 18874368 | bytes 6291456 | tf_op jit(solution)/shard_map/pallas_call | solution.py:79
  26.0 1.8 %fusion.14 = (bf16[256,2048]{1,0:T(8,128)(2,1)}, bf16[256,2048]{1,0:T(8,128)(2,1)}, bf16[256,2048]{1,0:T(8,128)(2,1)}) fusion(bf16[768,2048]{1,0:T(8,128)(2,1)S(1)} %shard_map.73), kind=kLoop, calls=%fused_computation.36 | loop fusion | bytes 6291456 | tf_op jit(solution)/shard_map/slice | solution.py:125
  27.8 7.7 %collective-permute-start.2 = (bf16[256,2048]{1,0:T(8,128)(2,1)}, bf16[256,2048]{1,0:T(8,128)(2,1)}, u32[]{:S(2)}, u32[]{:S(2)}) collective-permute-start(bf16[256,2048]{1,0:T(8,128)(2,1)} %get-tuple-element.7), channel_id=1, source_target_pairs={{0,1},{1,0},{2,3},{3,2},{4,5},{5,4},{6,7},{7,6},{8,9},{9,8},{10,11... | collective-permute-start | bytes 3145736 | tf_op jit(solution)/shard_map/ppermute | solution.py:125
  35.5 1.9 %collective-permute-start.3 = (bf16[256,2048]{1,0:T(8,128)(2,1)}, bf16[256,2048]{1,0:T(8,128)(2,1)}, u32[]{:S(2)}, u32[]{:S(2)}) collective-permute-start(bf16[256,2048]{1,0:T(8,128)(2,1)} %get-tuple-element.6), channel_id=1, source_target_pairs={{0,1},{1,0},{2,3},{3,2},{4,5},{5,4},{6,7},{7,6},{8,9},{9,8},{10,11... | collective-permute-start | bytes 3145736 | tf_op jit(solution)/shard_map/ppermute | solution.py:125
  37.4 2.4 %collective-permute-start.4 = (bf16[256,2048]{1,0:T(8,128)(2,1)}, bf16[256,2048]{1,0:T(8,128)(2,1)}, u32[]{:S(2)}, u32[]{:S(2)}) collective-permute-start(bf16[256,2048]{1,0:T(8,128)(2,1)} %get-tuple-element.5), channel_id=1, source_target_pairs={{0,1},{1,0},{2,3},{3,2},{4,5},{5,4},{6,7},{7,6},{8,9},{9,8},{10,11... | collective-permute-start | bytes 3145736 | tf_op jit(solution)/shard_map/ppermute | solution.py:125
  39.9 2.4 %collective-permute-done.1 = bf16[2,128,2048]{2,1,0:T(8,128)(2,1)} collective-permute-done((bf16[2,128,2048]{2,1,0:T(8,128)(2,1)}, bf16[2,128,2048]{2,1,0:T(8,128)(2,1)}, u32[]{:S(2)}, u32[]{:S(2)}) %collective-permute-start.1) | collective-permute-done | bytes 1048608 | tf_op jit(solution)/shard_map/ppermute | solution.py:130
  42.3 1.7 %broadcast_select_fusion.2 = bf16[2,128,2048]{2,1,0:T(8,128)(2,1)S(1)} fusion(bf16[2,128,2048]{2,1,0:T(8,128)(2,1)} %collective-permute-done.1, pred[]{:T(512)S(6)} %eq.3, bf16[1,128,2048]{2,1,0:T(8,128)(2,1)} %bitcast.50, bf16[1,128,2048]{2,1,0:T(8,128)(2,1)} %bitcast.47), kind=kLoop, calls=%fused_computation.16 | loop fusion | flops 1048576 | bytes 3145729 | tf_op jit(solution)/shard_map/jit(_where)/select_n | solution.py:139
  43.9 4.2 %collective-permute-start.5 = (bf16[2,128,2048]{2,1,0:T(8,128)(2,1)}, bf16[2,128,2048]{2,1,0:T(8,128)(2,1)S(1)}, u32[]{:S(2)}, u32[]{:S(2)}) collective-permute-start(bf16[2,128,2048]{2,1,0:T(8,128)(2,1)} %collective-permute-done.1), channel_id=1, source_target_pairs={{1,449},{3,451},{5,453},{7,455},{9,457},{11,459},{13,461},{15,463}... | collective-permute-start | bytes 3145736 | tf_op jit(solution)/shard_map/ppermute | solution.py:130
  48.1 0.0 collective-permute-done.7
  48.1 1.4 %collective-permute-start.8 = (bf16[2,128,2048]{2,1,0:T(8,128)(2,1)}, bf16[2,128,2048]{2,1,0:T(8,128)(2,1)S(1)}, u32[]{:S(2)}, u32[]{:S(2)}) collective-permute-start(bf16[2,128,2048]{2,1,0:T(8,128)(2,1)} %collective-permute-done.7), channel_id=1, source_target_pairs={{1,65},{3,67},{5,69},{7,71},{9,73},{11,75},{13,77},{15,79},{17,81}... | collective-permute-start | bytes 3145736 | tf_op jit(solution)/shard_map/ppermute | solution.py:129
  49.5 0.0 collective-permute-done.2
  49.5 1.3 %constant_dynamic-update-slice_fusion.2 = bf16[768,2048]{1,0:T(8,128)(2,1)S(1)} fusion(bf16[256,2048]{1,0:T(8,128)(2,1)} %collective-permute-done.2), kind=kLoop, calls=%fused_computation.32 | loop fusion | bytes 2097152
  50.8 0.0 collective-permute-done.3
  50.8 1.3 %constant_dynamic-update-slice_fusion.1 = bf16[768,2048]{1,0:T(8,128)(2,1)S(1)} fusion(bf16[768,2048]{1,0:T(8,128)(2,1)S(1)} %constant_dynamic-update-slice_fusion.2, bf16[256,2048]{1,0:T(8,128)(2,1)} %collective-permute-done.3), kind=kLoop, calls=%fused_computation.31 | loop fusion | bytes 2097152
  52.1 0.0 collective-permute-done.4
  52.1 1.3 %constant_dynamic-update-slice_fusion = bf16[768,2048]{1,0:T(8,128)(2,1)S(1)} fusion(bf16[768,2048]{1,0:T(8,128)(2,1)S(1)} %constant_dynamic-update-slice_fusion.1, bf16[256,2048]{1,0:T(8,128)(2,1)} %collective-permute-done.4), kind=kLoop, calls=%fused_computation.30 | loop fusion | bytes 2097152 | tf_op jit(solution)/shard_map/concatenate | solution.py:124
  53.4 1.2 fusion.11
  54.6 1.2 fusion.7
  55.8 6.3 %collective-permute-done.8 = bf16[2,128,2048]{2,1,0:T(8,128)(2,1)S(1)} collective-permute-done((bf16[2,128,2048]{2,1,0:T(8,128)(2,1)}, bf16[2,128,2048]{2,1,0:T(8,128)(2,1)S(1)}, u32[]{:S(2)}, u32[]{:S(2)}) %collective-permute-start.8) | collective-permute-done | bytes 1048608 | tf_op jit(solution)/shard_map/ppermute | solution.py:129
  62.0 1.3 %collective-permute-start.9 = (bf16[2,128,2048]{2,1,0:T(8,128)(2,1)S(1)}, bf16[2,128,2048]{2,1,0:T(8,128)(2,1)S(1)}, u32[]{:S(2)}, u32[]{:S(2)}) collective-permute-start(bf16[2,128,2048]{2,1,0:T(8,128)(2,1)S(1)} %collective-permute-done.8), channel_id=1, source_target_pairs={{0,64},{2,66},{4,68},{6,70},{8,72},{10,74},{12,76},{14,78},{16,80}... | collective-permute-start | bytes 3145736 | tf_op jit(solution)/shard_map/ppermute | solution.py:129
  63.3 0.0 collective-permute-done.5
  63.3 1.3 %collective-permute-start.6 = (bf16[2,128,2048]{2,1,0:T(8,128)(2,1)S(1)}, bf16[2,128,2048]{2,1,0:T(8,128)(2,1)S(1)}, u32[]{:S(2)}, u32[]{:S(2)}) collective-permute-start(bf16[2,128,2048]{2,1,0:T(8,128)(2,1)S(1)} %collective-permute-done.5), channel_id=1, source_target_pairs={{0,448},{2,450},{4,452},{6,454},{8,456},{10,458},{12,460},{14,462}... | collective-permute-start | bytes 3145736 | tf_op jit(solution)/shard_map/ppermute | solution.py:130
  64.6 1.4 %broadcast_select_fusion = bf16[2,128,2048]{2,1,0:T(8,128)(2,1)S(1)} fusion(bf16[2,128,2048]{2,1,0:T(8,128)(2,1)S(1)} %collective-permute-done.8, bf16[2,128,2048]{2,1,0:T(8,128)(2,1)} %collective-permute-done.7, pred[]{:T(512)S(6)} %eq.3), kind=kLoop, calls=%fused_computation.14 | loop fusion | flops 524288 | bytes 3145729 | tf_op jit(solution)/shard_map/jit(_where)/select_n | solution.py:142
  66.0 1.2 fusion.8
  67.2 1.2 fusion.4
  68.4 11.9 %collective-permute-done.6 = bf16[2,128,2048]{2,1,0:T(8,128)(2,1)S(1)} collective-permute-done((bf16[2,128,2048]{2,1,0:T(8,128)(2,1)S(1)}, bf16[2,128,2048]{2,1,0:T(8,128)(2,1)S(1)}, u32[]{:S(2)}, u32[]{:S(2)}) %collective-permute-start.6) | collective-permute-done | bytes 1048608 | tf_op jit(solution)/shard_map/ppermute | solution.py:130
  80.4 2.6 %collective-permute-start.11 = (bf16[2,64,2048]{2,1,0:T(8,128)(2,1)S(1)}, bf16[2,64,2048]{2,1,0:T(8,128)(2,1)S(1)}, u32[]{:S(2)}, u32[]{:S(2)}) collective-permute-start(bf16[2,64,2048]{2,1,0:T(8,128)(2,1)S(1)} %slice.65), channel_id=1, source_target_pairs={{1,449},{3,451},{5,453},{7,455},{9,457},{11,459},{13,461},{15,463}... | collective-permute-start | bytes 1572872 | tf_op jit(solution)/shard_map/ppermute | solution.py:134
  82.9 0.0 collective-permute-done.9
  83.0 1.3 %collective-permute-start.10 = (bf16[2,64,2048]{2,1,0:T(8,128)(2,1)S(1)}, bf16[2,64,2048]{2,1,0:T(8,128)(2,1)S(1)}, u32[]{:S(2)}, u32[]{:S(2)}) collective-permute-start(bf16[2,64,2048]{2,1,0:T(8,128)(2,1)S(1)} %slice.64), channel_id=1, source_target_pairs={{1,65},{3,67},{5,69},{7,71},{9,73},{11,75},{13,77},{15,79},{17,81}... | collective-permute-start | bytes 1572872 | tf_op jit(solution)/shard_map/ppermute | solution.py:133
  84.3 0.1 broadcast_select_fusion.1
  84.5 1.2 fusion.10
  85.6 1.2 fusion.6
  86.8 2.8 %collective-permute-done.11 = bf16[2,64,2048]{2,1,0:T(8,128)(2,1)S(1)} collective-permute-done((bf16[2,64,2048]{2,1,0:T(8,128)(2,1)S(1)}, bf16[2,64,2048]{2,1,0:T(8,128)(2,1)S(1)}, u32[]{:S(2)}, u32[]{:S(2)}) %collective-permute-start.11) | collective-permute-done | bytes 524320 | tf_op jit(solution)/shard_map/ppermute | solution.py:134
  89.6 1.4 %collective-permute-done.10 = bf16[2,64,2048]{2,1,0:T(8,128)(2,1)S(1)} collective-permute-done((bf16[2,64,2048]{2,1,0:T(8,128)(2,1)S(1)}, bf16[2,64,2048]{2,1,0:T(8,128)(2,1)S(1)}, u32[]{:S(2)}, u32[]{:S(2)}) %collective-permute-start.10) | collective-permute-done | bytes 524320 | tf_op jit(solution)/shard_map/ppermute | solution.py:133
  91.0 0.4 maximum_select_fusion
  91.4 1.2 fusion.9
  92.6 1.2 fusion.5
  93.8 0.1 pad_maximum_fusion.1
  93.9 26.6 %all_to_all.11 = bf16[4,128,768]{2,1,0:T(8,128)(2,1)S(1)} all-to-all(bf16[4,128,768]{2,1,0:T(8,128)(2,1)S(1)} %pad_maximum_fusion.1), channel_id=1, replica_groups={{0,2,4,6},{1,3,5,7},{8,10,12,14},{9,11,13,15},{16,18,20,22},{17,19,21,2..., dimensions={0} | all-to-all | bytes 1572864 | tf_op jit(solution)/shard_map/all_to_all | solution.py:146
  120.5 0.8 reduce_sum.12
  (5 shorter events, 0.1 us)
Async XLA Ops:
  0.0 22.9 %copy-start.7 = (f32[768]{0:T(1024)S(1)}, f32[768]{0:T(1024)}, u32[]{:S(2)}) copy-start(f32[768]{0:T(1024)} %param.11) | copy-start | bytes 9220
  0.0 22.9 %copy-start = (s32[768,1024]{1,0:T(8,128)S(1)}, s32[768,1024]{1,0:T(8,128)}, u32[]{:S(2)}) copy-start(s32[768,1024]{1,0:T(8,128)} %words_ref.1) | copy-start | bytes 9437188
  0.0 22.9 %copy-start.1 = (s32[6,2048]{1,0:T(8,128)S(1)}, s32[6,2048]{1,0:T(8,128)}, u32[]{:S(2)}) copy-start(s32[6,2048]{1,0:T(8,128)} %zero_ref.1) | copy-start | bytes 147460
  0.0 22.9 %copy-start.2 = (f32[6,2048]{1,0:T(8,128)S(1)}, f32[6,2048]{1,0:T(8,128)}, u32[]{:S(2)}) copy-start(f32[6,2048]{1,0:T(8,128)} %scale_ref.1) | copy-start | bytes 147460
  0.0 22.9 %copy-start.4 = (bf16[768,16]{0,1:T(8,128)(2,1)S(1)}, bf16[768,16]{0,1:T(8,128)(2,1)}, u32[]{:S(2)}) copy-start(bf16[768,16]{0,1:T(8,128)(2,1)} %param.12) | copy-start | bytes 73732
  0.0 22.9 %copy-start.3 = (bf16[16,2048]{1,0:T(8,128)(2,1)S(1)}, bf16[16,2048]{1,0:T(8,128)(2,1)}, u32[]{:S(2)}) copy-start(bf16[16,2048]{1,0:T(8,128)(2,1)} %up_ref.1) | copy-start | bytes 196612
  16.3 6.6 %copy-start.5 = (bf16[8,16,2048]{2,1,0:T(8,128)(2,1)}, bf16[8,16,2048]{2,1,0:T(8,128)(2,1)S(1)}, u32[]{:S(2)}) copy-start(bf16[8,16,2048]{2,1,0:T(8,128)(2,1)S(1)} %all_to_all.10) | copy-start | bytes 1572868
  16.3 2.8 %collective-permute-start = (bf16[128,2048]{1,0:T(8,128)(2,1)S(1)}, bf16[128,2048]{1,0:T(8,128)(2,1)S(1)}, u32[]{:S(2)}, u32[]{:S(2)}) collective-permute-start(bf16[128,2048]{1,0:T(8,128)(2,1)S(1)} %bitcast.45), channel_id=1, source_target_pairs={{1,0},{3,2},{5,4},{7,6},{9,8},{11,10},{13,12},{15,14},{17,16},{19,... | collective-permute-start | bytes 1572872 | tf_op jit(solution)/shard_map/ppermute | solution.py:121
  19.1 3.8 %copy-start.6 = (bf16[128,2048]{1,0:T(8,128)(2,1)}, bf16[128,2048]{1,0:T(8,128)(2,1)S(1)}, u32[]{:S(2)}) copy-start(bf16[128,2048]{1,0:T(8,128)(2,1)S(1)} %collective-permute-done) | copy-start | bytes 1572868
  20.3 27.8 %collective-permute-start.7 = (bf16[2,128,2048]{2,1,0:T(8,128)(2,1)}, bf16[2,128,2048]{2,1,0:T(8,128)(2,1)}, u32[]{:S(2)}, u32[]{:S(2)}) collective-permute-start(bf16[2,128,2048]{2,1,0:T(8,128)(2,1)} %pad_maximum_fusion), channel_id=1, source_target_pairs={{0,64},{2,66},{4,68},{6,70},{8,72},{10,74},{12,76},{14,78},{16,80}... | collective-permute-start | bytes 3145736 | tf_op jit(solution)/shard_map/ppermute | solution.py:129
  21.6 20.7 %collective-permute-start.1 = (bf16[2,128,2048]{2,1,0:T(8,128)(2,1)}, bf16[2,128,2048]{2,1,0:T(8,128)(2,1)}, u32[]{:S(2)}, u32[]{:S(2)}) collective-permute-start(bf16[2,128,2048]{2,1,0:T(8,128)(2,1)} %pad_maximum_fusion), channel_id=1, source_target_pairs={{0,448},{2,450},{4,452},{6,454},{8,456},{10,458},{12,460},{14,462}... | collective-permute-start | bytes 3145736 | tf_op jit(solution)/shard_map/ppermute | solution.py:130
  27.8 21.7 %collective-permute-start.2 = (bf16[256,2048]{1,0:T(8,128)(2,1)}, bf16[256,2048]{1,0:T(8,128)(2,1)}, u32[]{:S(2)}, u32[]{:S(2)}) collective-permute-start(bf16[256,2048]{1,0:T(8,128)(2,1)} %get-tuple-element.7), channel_id=1, source_target_pairs={{0,1},{1,0},{2,3},{3,2},{4,5},{5,4},{6,7},{7,6},{8,9},{9,8},{10,11... | collective-permute-start | bytes 3145736 | tf_op jit(solution)/shard_map/ppermute | solution.py:125
  35.5 15.3 %collective-permute-start.3 = (bf16[256,2048]{1,0:T(8,128)(2,1)}, bf16[256,2048]{1,0:T(8,128)(2,1)}, u32[]{:S(2)}, u32[]{:S(2)}) collective-permute-start(bf16[256,2048]{1,0:T(8,128)(2,1)} %get-tuple-element.6), channel_id=1, source_target_pairs={{0,1},{1,0},{2,3},{3,2},{4,5},{5,4},{6,7},{7,6},{8,9},{9,8},{10,11... | collective-permute-start | bytes 3145736 | tf_op jit(solution)/shard_map/ppermute | solution.py:125
  37.4 14.7 %collective-permute-start.4 = (bf16[256,2048]{1,0:T(8,128)(2,1)}, bf16[256,2048]{1,0:T(8,128)(2,1)}, u32[]{:S(2)}, u32[]{:S(2)}) collective-permute-start(bf16[256,2048]{1,0:T(8,128)(2,1)} %get-tuple-element.5), channel_id=1, source_target_pairs={{0,1},{1,0},{2,3},{3,2},{4,5},{5,4},{6,7},{7,6},{8,9},{9,8},{10,11... | collective-permute-start | bytes 3145736 | tf_op jit(solution)/shard_map/ppermute | solution.py:125
  43.9 19.4 %collective-permute-start.5 = (bf16[2,128,2048]{2,1,0:T(8,128)(2,1)}, bf16[2,128,2048]{2,1,0:T(8,128)(2,1)S(1)}, u32[]{:S(2)}, u32[]{:S(2)}) collective-permute-start(bf16[2,128,2048]{2,1,0:T(8,128)(2,1)} %collective-permute-done.1), channel_id=1, source_target_pairs={{1,449},{3,451},{5,453},{7,455},{9,457},{11,459},{13,461},{15,463}... | collective-permute-start | bytes 3145736 | tf_op jit(solution)/shard_map/ppermute | solution.py:130
  48.1 13.9 %collective-permute-start.8 = (bf16[2,128,2048]{2,1,0:T(8,128)(2,1)}, bf16[2,128,2048]{2,1,0:T(8,128)(2,1)S(1)}, u32[]{:S(2)}, u32[]{:S(2)}) collective-permute-start(bf16[2,128,2048]{2,1,0:T(8,128)(2,1)} %collective-permute-done.7), channel_id=1, source_target_pairs={{1,65},{3,67},{5,69},{7,71},{9,73},{11,75},{13,77},{15,79},{17,81}... | collective-permute-start | bytes 3145736 | tf_op jit(solution)/shard_map/ppermute | solution.py:129
  62.0 20.9 %collective-permute-start.9 = (bf16[2,128,2048]{2,1,0:T(8,128)(2,1)S(1)}, bf16[2,128,2048]{2,1,0:T(8,128)(2,1)S(1)}, u32[]{:S(2)}, u32[]{:S(2)}) collective-permute-start(bf16[2,128,2048]{2,1,0:T(8,128)(2,1)S(1)} %collective-permute-done.8), channel_id=1, source_target_pairs={{0,64},{2,66},{4,68},{6,70},{8,72},{10,74},{12,76},{14,78},{16,80}... | collective-permute-start | bytes 3145736 | tf_op jit(solution)/shard_map/ppermute | solution.py:129
  63.3 17.0 %collective-permute-start.6 = (bf16[2,128,2048]{2,1,0:T(8,128)(2,1)S(1)}, bf16[2,128,2048]{2,1,0:T(8,128)(2,1)S(1)}, u32[]{:S(2)}, u32[]{:S(2)}) collective-permute-start(bf16[2,128,2048]{2,1,0:T(8,128)(2,1)S(1)} %collective-permute-done.5), channel_id=1, source_target_pairs={{0,448},{2,450},{4,452},{6,454},{8,456},{10,458},{12,460},{14,462}... | collective-permute-start | bytes 3145736 | tf_op jit(solution)/shard_map/ppermute | solution.py:130
  80.4 9.2 %collective-permute-start.11 = (bf16[2,64,2048]{2,1,0:T(8,128)(2,1)S(1)}, bf16[2,64,2048]{2,1,0:T(8,128)(2,1)S(1)}, u32[]{:S(2)}, u32[]{:S(2)}) collective-permute-start(bf16[2,64,2048]{2,1,0:T(8,128)(2,1)S(1)} %slice.65), channel_id=1, source_target_pairs={{1,449},{3,451},{5,453},{7,455},{9,457},{11,459},{13,461},{15,463}... | collective-permute-start | bytes 1572872 | tf_op jit(solution)/shard_map/ppermute | solution.py:134
  83.0 8.0 %collective-permute-start.10 = (bf16[2,64,2048]{2,1,0:T(8,128)(2,1)S(1)}, bf16[2,64,2048]{2,1,0:T(8,128)(2,1)S(1)}, u32[]{:S(2)}, u32[]{:S(2)}) collective-permute-start(bf16[2,64,2048]{2,1,0:T(8,128)(2,1)S(1)} %slice.64), channel_id=1, source_target_pairs={{1,65},{3,67},{5,69},{7,71},{9,73},{11,75},{13,77},{15,79},{17,81}... | collective-permute-start | bytes 1572872 | tf_op jit(solution)/shard_map/ppermute | solution.py:133

commit v2 on v1

--- a/solution.py
+++ b/solution.py
@@ -141,8 +141,11 @@
         jnp.where(home, far, low[3]),
         jnp.where(home, low[2], low[1]),
     ]
-    blocks = [lax.optimization_barrier(block) for block in blocks]
-    parts = jnp.stack([times(block, weight, other_weight).astype(jnp.bfloat16) for block in blocks])
+    blocks[1:3] = [lax.optimization_barrier(block) for block in blocks[1:3]]
+    pair = jnp.concatenate([blocks[0], blocks[3]], 1)
+    pair = times(pair, weight, other_weight).astype(jnp.bfloat16)
+    middle = [times(block, weight, other_weight).astype(jnp.bfloat16) for block in blocks[1:3]]
+    parts = jnp.stack([pair[:tokens], *middle, pair[tokens:]])
     parts = lax.all_to_all(parts, BOTH, 0, 0, axis_index_groups=OWNERS)
     return jnp.sum(parts.astype(jnp.float32), axis=0).astype(jnp.bfloat16)
 

time: 122 us -> 119 us (0.975)
  waiting for transfers between devices: 26.3 us -> 23.5 us
  matrix products: 9.4 us -> 6.95 us
  starting transfers between devices: 27.9 us -> 30.3 us
    ppermute x3, waiting for transfers between devices: 6.26 us -> 2.99 us  [shards(): low.append(lax.ppermute(low[-1], BOTH, hop(1, step % 2 == 0)))]
    ppermute x3, starting transfers between devices: 3.92 us -> 6.2 us  [shards(): low.append(lax.ppermute(low[-1], BOTH, hop(1, step % 2 == 0)))]
    dot_general x4 -> x3, matrix products: 4.7 us -> 3.45 us  [times(): lax.dot_general(block[1], other_weight, dims, preferred_element_type=jnp....]
    dot_general x4 -> x3, matrix products: 4.7 us -> 3.5 us  [times(): lax.dot_general(block[0], weight, dims, preferred_element_type=jnp.float32)]
    unnamed x18 -> x22, local copies, waits for them, and re-layouts: 2.62 us -> 2.63 us
  transfers between devices with their start and end apart: 12 -> 12, of which waited for: 6 -> 6; matrix products, arithmetic and copies ran while one was open for 13% -> 11% of each run, Pallas kernels for 2% -> 3%
where the time goes in v2:
time: 119 us
  blocking collectives  42.1 us (35%)
  starting transfers between devices  30.3 us (25%)
  waiting for transfers between devices  23.5 us (20%)
  matrix products  6.95 us (6%)
  local copies, waits for them, and re-layouts  6.86 us (6%)
  other arithmetic  5.32 us (4%)
  Pallas kernels  3.07 us (3%)
    all_to_all x1, blocking collectives, shards(): parts = lax.all_to_all(parts, BOTH, 0, 0, axis_index_groups=OWNERS)  26.9 us
    all_to_all x1, blocking collectives, send_all(): return lax.all_to_all(copies, 'wide', 0, 0, axis_index_groups=groups)  15.2 us
    ppermute x3, waiting for transfers between devices, shards(): high.append(lax.ppermute(high[-1], BOTH, hop(-1, step % 2 == 0)))  14.9 us
    ppermute x3, starting transfers between devices, shards(): lax.ppermute(weight[i:i + 256], 'narrow', OTHER_CORE)  12 us
    ppermute x3, starting transfers between devices, shards(): high.append(lax.ppermute(high[-1], BOTH, hop(-1, step % 2 == 0)))  6.8 us
    ppermute x3, starting transfers between devices, shards(): low.append(lax.ppermute(low[-1], BOTH, hop(1, step % 2 == 0)))  6.2 us
    dot_general x3, matrix products, times(): lax.dot_general(block[0], weight, dims, preferred_element_type=jnp.float32)  3.5 us
    dot_general x3, matrix products, times(): lax.dot_general(block[1], other_weight, dims, preferred_element_type=jnp....  3.45 us
  transfers between devices with their start and end apart: 12, of which 6 were waited for; matrix products, arithmetic and copies ran while one was open for 11% of the time, Pallas kernels for 3%

profile of v2, /device:TPU:64, one launch (start us, length us, event | category | flops | bytes accessed | tf_op | source)
XLA Modules:
  0.0 118.5 jit_solution(16966703377458544047)
XLA Ops:
  0.0 0.0 copy-start.9
  0.0 0.0 copy-start
  0.0 0.0 copy-start.1
  0.0 0.0 copy-start.2
  0.0 0.0 copy-start.4
  0.0 0.0 copy-start.3
  0.0 1.0 broadcast_in_dim.2
  1.1 15.2 %all_to_all.10 = bf16[8,16,2048]{2,1,0:T(8,128)(2,1)S(1)} all-to-all(bf16[8,16,2048]{2,1,0:T(8,128)(2,1)S(1)} %broadcast_in_dim.2), channel_id=1, replica_groups={{0,8,16,24,32,40,48,56},{64,72,80,88,96,104,112,120},{128,136,144,152,1..., dimensions={0} | all-to-all | bytes 1048576 | tf_op jit(solution)/shard_map/all_to_all | solution.py:101
  16.3 0.0 copy-start.5
  16.3 1.3 %collective-permute-start = (bf16[128,2048]{1,0:T(8,128)(2,1)S(1)}, bf16[128,2048]{1,0:T(8,128)(2,1)S(1)}, u32[]{:S(2)}, u32[]{:S(2)}) collective-permute-start(bf16[128,2048]{1,0:T(8,128)(2,1)S(1)} %bitcast.41), channel_id=1, source_target_pairs={{1,0},{3,2},{5,4},{7,6},{9,8},{11,10},{13,12},{15,14},{17,16},{19,... | collective-permute-start | bytes 1572872 | tf_op jit(solution)/shard_map/ppermute | solution.py:121
  17.6 1.5 %collective-permute-done = bf16[128,2048]{1,0:T(8,128)(2,1)S(1)} collective-permute-done((bf16[128,2048]{1,0:T(8,128)(2,1)S(1)}, bf16[128,2048]{1,0:T(8,128)(2,1)S(1)}, u32[]{:S(2)}, u32[]{:S(2)}) %collective-permute-start) | collective-permute-done | bytes 524320 | tf_op jit(solution)/shard_map/ppermute | solution.py:121
  19.1 1.2 pad_maximum_fusion.1
  20.3 1.3 %collective-permute-start.2 = (bf16[2,128,2048]{2,1,0:T(8,128)(2,1)}, bf16[2,128,2048]{2,1,0:T(8,128)(2,1)}, u32[]{:S(2)}, u32[]{:S(2)}) collective-permute-start(bf16[2,128,2048]{2,1,0:T(8,128)(2,1)} %pad_maximum_fusion.1), channel_id=1, source_target_pairs={{0,64},{2,66},{4,68},{6,70},{8,72},{10,74},{12,76},{14,78},{16,80}... | collective-permute-start | bytes 3145736 | tf_op jit(solution)/shard_map/ppermute | solution.py:129
  21.6 1.3 %collective-permute-start.1 = (bf16[2,128,2048]{2,1,0:T(8,128)(2,1)}, bf16[2,128,2048]{2,1,0:T(8,128)(2,1)}, u32[]{:S(2)}, u32[]{:S(2)}) collective-permute-start(bf16[2,128,2048]{2,1,0:T(8,128)(2,1)} %pad_maximum_fusion.1), channel_id=1, source_target_pairs={{0,448},{2,450},{4,452},{6,454},{8,456},{10,458},{12,460},{14,462}... | collective-permute-start | bytes 3145736 | tf_op jit(solution)/shard_map/ppermute | solution.py:130
  22.9 0.0 copy-done.9
  22.9 0.0 copy-done.5
  22.9 0.0 copy-done.7
  22.9 0.0 copy-done
  23.0 0.0 copy-done.1
  23.0 0.0 copy-done.2
  23.0 0.0 copy-done.4
  23.0 0.0 copy-done.3
  23.0 3.1 %shard_map.73 = bf16[768,2048]{1,0:T(8,128)(2,1)S(1)} custom-call(s32[768,1024]{1,0:T(8,128)S(1)} %copy-done, s32[6,2048]{1,0:T(8,128)S(1)} %copy-done.1, f32[6,2048]{1,0:T(8,128)S(1)} %copy-done.2, f32[1,768]{1,0:T(1,128)S(1)} %reshape.11.channel_ref, bf16[16,768]{1,0:T(8,128)(2,1)S(1)} %bitcast.40, bf16[16,2048]{1,0:T(8,128)(2,1)S(1)} %copy-done.3), custom_call_target="tpu_custom_call" | custom-call | flops 18874368 | bytes 6291456 | tf_op jit(solution)/shard_map/pallas_call | solution.py:79
  26.1 1.8 %fusion.24 = (bf16[256,2048]{1,0:T(8,128)(2,1)}, bf16[256,2048]{1,0:T(8,128)(2,1)}, bf16[256,2048]{1,0:T(8,128)(2,1)}) fusion(bf16[768,2048]{1,0:T(8,128)(2,1)S(1)} %shard_map.73), kind=kLoop, calls=%fused_computation.39 | loop fusion | bytes 6291456 | tf_op jit(solution)/shard_map/slice | solution.py:125
  27.9 7.7 %collective-permute-start.4 = (bf16[256,2048]{1,0:T(8,128)(2,1)}, bf16[256,2048]{1,0:T(8,128)(2,1)}, u32[]{:S(2)}, u32[]{:S(2)}) collective-permute-start(bf16[256,2048]{1,0:T(8,128)(2,1)} %get-tuple-element.7), channel_id=1, source_target_pairs={{0,1},{1,0},{2,3},{3,2},{4,5},{5,4},{6,7},{7,6},{8,9},{9,8},{10,11... | collective-permute-start | bytes 3145736 | tf_op jit(solution)/shard_map/ppermute | solution.py:125
  35.5 1.9 %collective-permute-start.5 = (bf16[256,2048]{1,0:T(8,128)(2,1)}, bf16[256,2048]{1,0:T(8,128)(2,1)}, u32[]{:S(2)}, u32[]{:S(2)}) collective-permute-start(bf16[256,2048]{1,0:T(8,128)(2,1)} %get-tuple-element.6), channel_id=1, source_target_pairs={{0,1},{1,0},{2,3},{3,2},{4,5},{5,4},{6,7},{7,6},{8,9},{9,8},{10,11... | collective-permute-start | bytes 3145736 | tf_op jit(solution)/shard_map/ppermute | solution.py:125
  37.5 2.4 %collective-permute-start.6 = (bf16[256,2048]{1,0:T(8,128)(2,1)}, bf16[256,2048]{1,0:T(8,128)(2,1)}, u32[]{:S(2)}, u32[]{:S(2)}) collective-permute-start(bf16[256,2048]{1,0:T(8,128)(2,1)} %get-tuple-element.5), channel_id=1, source_target_pairs={{0,1},{1,0},{2,3},{3,2},{4,5},{5,4},{6,7},{7,6},{8,9},{9,8},{10,11... | collective-permute-start | bytes 3145736 | tf_op jit(solution)/shard_map/ppermute | solution.py:125
  39.9 0.0 copy-start.6
  39.9 0.0 copy-start.8
  39.9 0.0 collective-permute-done.2
  39.9 3.6 %collective-permute-start.3 = (bf16[2,128,2048]{2,1,0:T(8,128)(2,1)}, bf16[2,128,2048]{2,1,0:T(8,128)(2,1)S(1)}, u32[]{:S(2)}, u32[]{:S(2)}) collective-permute-start(bf16[2,128,2048]{2,1,0:T(8,128)(2,1)} %collective-permute-done.2), channel_id=1, source_target_pairs={{1,65},{3,67},{5,69},{7,71},{9,73},{11,75},{13,77},{15,79},{17,81}... | collective-permute-start | bytes 3145736 | tf_op jit(solution)/shard_map/ppermute | solution.py:129
  43.6 0.0 collective-permute-done.1
  43.6 4.2 %collective-permute-start.7 = (bf16[2,128,2048]{2,1,0:T(8,128)(2,1)}, bf16[2,128,2048]{2,1,0:T(8,128)(2,1)S(1)}, u32[]{:S(2)}, u32[]{:S(2)}) collective-permute-start(bf16[2,128,2048]{2,1,0:T(8,128)(2,1)} %collective-permute-done.1), channel_id=1, source_target_pairs={{1,449},{3,451},{5,453},{7,455},{9,457},{11,459},{13,461},{15,463}... | collective-permute-start | bytes 3145736 | tf_op jit(solution)/shard_map/ppermute | solution.py:130
  47.8 0.0 collective-permute-done.4
  47.8 1.3 %constant_dynamic-update-slice_fusion.2 = bf16[768,2048]{1,0:T(8,128)(2,1)S(1)} fusion(bf16[256,2048]{1,0:T(8,128)(2,1)} %collective-permute-done.4), kind=kLoop, calls=%fused_computation.33 | loop fusion | bytes 2097152
  49.1 0.0 collective-permute-done.5
  49.1 1.3 %constant_dynamic-update-slice_fusion.1 = bf16[768,2048]{1,0:T(8,128)(2,1)S(1)} fusion(bf16[768,2048]{1,0:T(8,128)(2,1)S(1)} %constant_dynamic-update-slice_fusion.2, bf16[256,2048]{1,0:T(8,128)(2,1)} %collective-permute-done.5), kind=kLoop, calls=%fused_computation.32 | loop fusion | bytes 2097152
  50.4 0.0 collective-permute-done.6
  50.5 1.3 %constant_dynamic-update-slice_fusion = bf16[768,2048]{1,0:T(8,128)(2,1)S(1)} fusion(bf16[768,2048]{1,0:T(8,128)(2,1)S(1)} %constant_dynamic-update-slice_fusion.1, bf16[256,2048]{1,0:T(8,128)(2,1)} %collective-permute-done.6), kind=kLoop, calls=%fused_computation.31 | loop fusion | bytes 2097152 | tf_op jit(solution)/shard_map/concatenate | solution.py:124
  51.7 0.0 copy-done.6
  51.8 0.0 copy-done.8
  51.8 1.4 %broadcast_select_fusion.2 = bf16[2,128,2048]{2,1,0:T(8,128)(2,1)S(1)} fusion(bf16[2,128,2048]{2,1,0:T(8,128)(2,1)} %collective-permute-done.1, pred[]{:T(512)S(6)} %eq.3, bf16[1,128,2048]{2,1,0:T(8,128)(2,1)S(1)} %bitcast.46, bf16[1,128,2048]{2,1,0:T(8,128)(2,1)S(1)} %bitcast.43), kind=kLoop, calls=%fused_computation.21 | loop fusion | flops 1048576 | bytes 3145729 | tf_op jit(solution)/shard_map/jit(_where)/select_n | solution.py:139
  53.1 3.0 %collective-permute-done.3 = bf16[2,128,2048]{2,1,0:T(8,128)(2,1)S(1)} collective-permute-done((bf16[2,128,2048]{2,1,0:T(8,128)(2,1)}, bf16[2,128,2048]{2,1,0:T(8,128)(2,1)S(1)}, u32[]{:S(2)}, u32[]{:S(2)}) %collective-permute-start.3) | collective-permute-done | bytes 1048608 | tf_op jit(solution)/shard_map/ppermute | solution.py:129
  56.1 1.3 %collective-permute-start.9 = (bf16[2,128,2048]{2,1,0:T(8,128)(2,1)S(1)}, bf16[2,128,2048]{2,1,0:T(8,128)(2,1)S(1)}, u32[]{:S(2)}, u32[]{:S(2)}) collective-permute-start(bf16[2,128,2048]{2,1,0:T(8,128)(2,1)S(1)} %collective-permute-done.3), channel_id=1, source_target_pairs={{0,64},{2,66},{4,68},{6,70},{8,72},{10,74},{12,76},{14,78},{16,80}... | collective-permute-start | bytes 3145736 | tf_op jit(solution)/shard_map/ppermute | solution.py:129
  57.4 3.0 %collective-permute-done.7 = bf16[2,128,2048]{2,1,0:T(8,128)(2,1)S(1)} collective-permute-done((bf16[2,128,2048]{2,1,0:T(8,128)(2,1)}, bf16[2,128,2048]{2,1,0:T(8,128)(2,1)S(1)}, u32[]{:S(2)}, u32[]{:S(2)}) %collective-permute-start.7) | collective-permute-done | bytes 1048608 | tf_op jit(solution)/shard_map/ppermute | solution.py:130
  60.4 1.3 %collective-permute-start.8 = (bf16[2,128,2048]{2,1,0:T(8,128)(2,1)S(1)}, bf16[2,128,2048]{2,1,0:T(8,128)(2,1)S(1)}, u32[]{:S(2)}, u32[]{:S(2)}) collective-permute-start(bf16[2,128,2048]{2,1,0:T(8,128)(2,1)S(1)} %collective-permute-done.7), channel_id=1, source_target_pairs={{0,448},{2,450},{4,452},{6,454},{8,456},{10,458},{12,460},{14,462}... | collective-permute-start | bytes 3145736 | tf_op jit(solution)/shard_map/ppermute | solution.py:130
  61.7 1.3 %broadcast_select_fusion.1 = bf16[2,128,2048]{2,1,0:T(8,128)(2,1)S(1)} fusion(bf16[2,128,2048]{2,1,0:T(8,128)(2,1)S(1)} %collective-permute-done.3, bf16[2,128,2048]{2,1,0:T(8,128)(2,1)} %collective-permute-done.2, pred[]{:T(512)S(6)} %eq.3), kind=kLoop, calls=%fused_computation.20 | loop fusion | flops 524288 | bytes 3145729 | tf_op jit(solution)/shard_map/jit(_where)/select_n | solution.py:142
  63.0 1.0 fusion.15
  64.0 1.1 fusion.11
  65.2 11.9 %collective-permute-done.8 = bf16[2,128,2048]{2,1,0:T(8,128)(2,1)S(1)} collective-permute-done((bf16[2,128,2048]{2,1,0:T(8,128)(2,1)S(1)}, bf16[2,128,2048]{2,1,0:T(8,128)(2,1)S(1)}, u32[]{:S(2)}, u32[]{:S(2)}) %collective-permute-start.8) | collective-permute-done | bytes 1048608 | tf_op jit(solution)/shard_map/ppermute | solution.py:130
  77.2 2.7 %collective-permute-start.11 = (bf16[2,64,2048]{2,1,0:T(8,128)(2,1)S(1)}, bf16[2,64,2048]{2,1,0:T(8,128)(2,1)S(1)}, u32[]{:S(2)}, u32[]{:S(2)}) collective-permute-start(bf16[2,64,2048]{2,1,0:T(8,128)(2,1)S(1)} %slice.66), channel_id=1, source_target_pairs={{1,449},{3,451},{5,453},{7,455},{9,457},{11,459},{13,461},{15,463}... | collective-permute-start | bytes 1572872 | tf_op jit(solution)/shard_map/ppermute | solution.py:134
  79.9 0.0 collective-permute-done.9
  79.9 1.3 %collective-permute-start.10 = (bf16[2,64,2048]{2,1,0:T(8,128)(2,1)S(1)}, bf16[2,64,2048]{2,1,0:T(8,128)(2,1)S(1)}, u32[]{:S(2)}, u32[]{:S(2)}) collective-permute-start(bf16[2,64,2048]{2,1,0:T(8,128)(2,1)S(1)} %slice.65), channel_id=1, source_target_pairs={{1,65},{3,67},{5,69},{7,71},{9,73},{11,75},{13,77},{15,79},{17,81}... | collective-permute-start | bytes 1572872 | tf_op jit(solution)/shard_map/ppermute | solution.py:133
  81.3 0.1 broadcast_select_fusion
  81.4 1.2 %fusion.19 = f32[128,768]{1,0:T(8,128)S(1)} fusion(bf16[768,2048]{1,0:T(8,128)(2,1)S(1)} %constant_dynamic-update-slice_fusion, bf16[2,128,2048]{2,1,0:T(8,128)(2,1)S(1)} %broadcast_select_fusion), kind=kOutput, calls=%fused_computation.27 | convolution fusion | flops 402653184 | bytes 4063232 | tf_op jit(solution)/shard_map/dot_general | solution.py:106
  82.6 1.2 fusion.3
  83.8 2.7 %collective-permute-done.11 = bf16[2,64,2048]{2,1,0:T(8,128)(2,1)S(1)} collective-permute-done((bf16[2,64,2048]{2,1,0:T(8,128)(2,1)S(1)}, bf16[2,64,2048]{2,1,0:T(8,128)(2,1)S(1)}, u32[]{:S(2)}, u32[]{:S(2)}) %collective-permute-start.11) | collective-permute-done | bytes 524320 | tf_op jit(solution)/shard_map/ppermute | solution.py:134
  86.5 1.4 %collective-permute-done.10 = bf16[2,64,2048]{2,1,0:T(8,128)(2,1)S(1)} collective-permute-done((bf16[2,64,2048]{2,1,0:T(8,128)(2,1)S(1)}, bf16[2,64,2048]{2,1,0:T(8,128)(2,1)S(1)}, u32[]{:S(2)}, u32[]{:S(2)}) %collective-permute-start.10) | collective-permute-done | bytes 524320 | tf_op jit(solution)/shard_map/ppermute | solution.py:133
  87.9 0.4 maximum_select_fusion
  88.3 1.2 %fusion.18 = f32[128,768]{1,0:T(8,128)S(1)} fusion(bf16[768,2048]{1,0:T(8,128)(2,1)S(1)} %constant_dynamic-update-slice_fusion, bf16[2,128,2048]{2,1,0:T(8,128)(2,1)S(1)} %maximum_select_fusion), kind=kOutput, calls=%fused_computation.24 | convolution fusion | flops 402653184 | bytes 4063232 | tf_op jit(solution)/shard_map/dot_general | solution.py:106
  89.5 1.2 fusion.2
  90.7 0.1 pad_maximum_fusion.2
  90.8 26.9 %all_to_all.11 = bf16[4,128,768]{2,1,0:T(8,128)(2,1)S(1)} all-to-all(bf16[4,128,768]{2,1,0:T(8,128)(2,1)S(1)} %pad_maximum_fusion.2), channel_id=1, replica_groups={{0,2,4,6},{1,3,5,7},{8,10,12,14},{9,11,13,15},{16,18,20,22},{17,19,21,2..., dimensions={0} | all-to-all | bytes 1572864 | tf_op jit(solution)/shard_map/all_to_all | solution.py:149
  117.7 0.8 reduce_sum.12
  (7 shorter events, 0.1 us)
Async XLA Ops:
  0.0 22.9 %copy-start.9 = (f32[768]{0:T(1024)S(1)}, f32[768]{0:T(1024)}, u32[]{:S(2)}) copy-start(f32[768]{0:T(1024)} %param.11) | copy-start | bytes 9220
  0.0 22.9 %copy-start = (s32[768,1024]{1,0:T(8,128)S(1)}, s32[768,1024]{1,0:T(8,128)}, u32[]{:S(2)}) copy-start(s32[768,1024]{1,0:T(8,128)} %words_ref.1) | copy-start | bytes 9437188
  0.0 22.9 %copy-start.1 = (s32[6,2048]{1,0:T(8,128)S(1)}, s32[6,2048]{1,0:T(8,128)}, u32[]{:S(2)}) copy-start(s32[6,2048]{1,0:T(8,128)} %zero_ref.1) | copy-start | bytes 147460
  0.0 23.0 %copy-start.2 = (f32[6,2048]{1,0:T(8,128)S(1)}, f32[6,2048]{1,0:T(8,128)}, u32[]{:S(2)}) copy-start(f32[6,2048]{1,0:T(8,128)} %scale_ref.1) | copy-start | bytes 147460
  0.0 23.0 %copy-start.4 = (bf16[768,16]{0,1:T(8,128)(2,1)S(1)}, bf16[768,16]{0,1:T(8,128)(2,1)}, u32[]{:S(2)}) copy-start(bf16[768,16]{0,1:T(8,128)(2,1)} %param.12) | copy-start | bytes 73732
  0.0 23.0 %copy-start.3 = (bf16[16,2048]{1,0:T(8,128)(2,1)S(1)}, bf16[16,2048]{1,0:T(8,128)(2,1)}, u32[]{:S(2)}) copy-start(bf16[16,2048]{1,0:T(8,128)(2,1)} %up_ref.1) | copy-start | bytes 196612
  16.3 6.6 %copy-start.5 = (bf16[8,16,2048]{2,1,0:T(8,128)(2,1)}, bf16[8,16,2048]{2,1,0:T(8,128)(2,1)S(1)}, u32[]{:S(2)}) copy-start(bf16[8,16,2048]{2,1,0:T(8,128)(2,1)S(1)} %all_to_all.10) | copy-start | bytes 1572868
  16.3 2.8 %collective-permute-start = (bf16[128,2048]{1,0:T(8,128)(2,1)S(1)}, bf16[128,2048]{1,0:T(8,128)(2,1)S(1)}, u32[]{:S(2)}, u32[]{:S(2)}) collective-permute-start(bf16[128,2048]{1,0:T(8,128)(2,1)S(1)} %bitcast.41), channel_id=1, source_target_pairs={{1,0},{3,2},{5,4},{7,6},{9,8},{11,10},{13,12},{15,14},{17,16},{19,... | collective-permute-start | bytes 1572872 | tf_op jit(solution)/shard_map/ppermute | solution.py:121
  19.1 3.8 %copy-start.7 = (bf16[128,2048]{1,0:T(8,128)(2,1)}, bf16[128,2048]{1,0:T(8,128)(2,1)S(1)}, u32[]{:S(2)}) copy-start(bf16[128,2048]{1,0:T(8,128)(2,1)S(1)} %collective-permute-done) | copy-start | bytes 1572868
  20.3 19.6 %collective-permute-start.2 = (bf16[2,128,2048]{2,1,0:T(8,128)(2,1)}, bf16[2,128,2048]{2,1,0:T(8,128)(2,1)}, u32[]{:S(2)}, u32[]{:S(2)}) collective-permute-start(bf16[2,128,2048]{2,1,0:T(8,128)(2,1)} %pad_maximum_fusion.1), channel_id=1, source_target_pairs={{0,64},{2,66},{4,68},{6,70},{8,72},{10,74},{12,76},{14,78},{16,80}... | collective-permute-start | bytes 3145736 | tf_op jit(solution)/shard_map/ppermute | solution.py:129
  21.6 22.0 %collective-permute-start.1 = (bf16[2,128,2048]{2,1,0:T(8,128)(2,1)}, bf16[2,128,2048]{2,1,0:T(8,128)(2,1)}, u32[]{:S(2)}, u32[]{:S(2)}) collective-permute-start(bf16[2,128,2048]{2,1,0:T(8,128)(2,1)} %pad_maximum_fusion.1), channel_id=1, source_target_pairs={{0,448},{2,450},{4,452},{6,454},{8,456},{10,458},{12,460},{14,462}... | collective-permute-start | bytes 3145736 | tf_op jit(solution)/shard_map/ppermute | solution.py:130
  27.9 20.0 %collective-permute-start.4 = (bf16[256,2048]{1,0:T(8,128)(2,1)}, bf16[256,2048]{1,0:T(8,128)(2,1)}, u32[]{:S(2)}, u32[]{:S(2)}) collective-permute-start(bf16[256,2048]{1,0:T(8,128)(2,1)} %get-tuple-element.7), channel_id=1, source_target_pairs={{0,1},{1,0},{2,3},{3,2},{4,5},{5,4},{6,7},{7,6},{8,9},{9,8},{10,11... | collective-permute-start | bytes 3145736 | tf_op jit(solution)/shard_map/ppermute | solution.py:125
  35.5 13.6 %collective-permute-start.5 = (bf16[256,2048]{1,0:T(8,128)(2,1)}, bf16[256,2048]{1,0:T(8,128)(2,1)}, u32[]{:S(2)}, u32[]{:S(2)}) collective-permute-start(bf16[256,2048]{1,0:T(8,128)(2,1)} %get-tuple-element.6), channel_id=1, source_target_pairs={{0,1},{1,0},{2,3},{3,2},{4,5},{5,4},{6,7},{7,6},{8,9},{9,8},{10,11... | collective-permute-start | bytes 3145736 | tf_op jit(solution)/shard_map/ppermute | solution.py:125
  37.5 13.0 %collective-permute-start.6 = (bf16[256,2048]{1,0:T(8,128)(2,1)}, bf16[256,2048]{1,0:T(8,128)(2,1)}, u32[]{:S(2)}, u32[]{:S(2)}) collective-permute-start(bf16[256,2048]{1,0:T(8,128)(2,1)} %get-tuple-element.5), channel_id=1, source_target_pairs={{0,1},{1,0},{2,3},{3,2},{4,5},{5,4},{6,7},{7,6},{8,9},{9,8},{10,11... | collective-permute-start | bytes 3145736 | tf_op jit(solution)/shard_map/ppermute | solution.py:125
  39.9 11.9 %copy-start.6 = (bf16[8,16,2048]{2,1,0:T(8,128)(2,1)S(1)}, bf16[8,16,2048]{2,1,0:T(8,128)(2,1)}, u32[]{:S(2)}) copy-start(bf16[8,16,2048]{2,1,0:T(8,128)(2,1)} %copy-done.5) | copy-start | bytes 1572868
  39.9 11.9 %copy-start.8 = (bf16[128,2048]{1,0:T(8,128)(2,1)S(1)}, bf16[128,2048]{1,0:T(8,128)(2,1)}, u32[]{:S(2)}) copy-start(bf16[128,2048]{1,0:T(8,128)(2,1)} %copy-done.7) | copy-start | bytes 1572868
  39.9 16.2 %collective-permute-start.3 = (bf16[2,128,2048]{2,1,0:T(8,128)(2,1)}, bf16[2,128,2048]{2,1,0:T(8,128)(2,1)S(1)}, u32[]{:S(2)}, u32[]{:S(2)}) collective-permute-start(bf16[2,128,2048]{2,1,0:T(8,128)(2,1)} %collective-permute-done.2), channel_id=1, source_target_pairs={{1,65},{3,67},{5,69},{7,71},{9,73},{11,75},{13,77},{15,79},{17,81}... | collective-permute-start | bytes 3145736 | tf_op jit(solution)/shard_map/ppermute | solution.py:129
  43.6 16.8 %collective-permute-start.7 = (bf16[2,128,2048]{2,1,0:T(8,128)(2,1)}, bf16[2,128,2048]{2,1,0:T(8,128)(2,1)S(1)}, u32[]{:S(2)}, u32[]{:S(2)}) collective-permute-start(bf16[2,128,2048]{2,1,0:T(8,128)(2,1)} %collective-permute-done.1), channel_id=1, source_target_pairs={{1,449},{3,451},{5,453},{7,455},{9,457},{11,459},{13,461},{15,463}... | collective-permute-start | bytes 3145736 | tf_op jit(solution)/shard_map/ppermute | solution.py:130
  56.1 23.7 %collective-permute-start.9 = (bf16[2,128,2048]{2,1,0:T(8,128)(2,1)S(1)}, bf16[2,128,2048]{2,1,0:T(8,128)(2,1)S(1)}, u32[]{:S(2)}, u32[]{:S(2)}) collective-permute-start(bf16[2,128,2048]{2,1,0:T(8,128)(2,1)S(1)} %collective-permute-done.3), channel_id=1, source_target_pairs={{0,64},{2,66},{4,68},{6,70},{8,72},{10,74},{12,76},{14,78},{16,80}... | collective-permute-start | bytes 3145736 | tf_op jit(solution)/shard_map/ppermute | solution.py:129
  60.4 16.8 %collective-permute-start.8 = (bf16[2,128,2048]{2,1,0:T(8,128)(2,1)S(1)}, bf16[2,128,2048]{2,1,0:T(8,128)(2,1)S(1)}, u32[]{:S(2)}, u32[]{:S(2)}) collective-permute-start(bf16[2,128,2048]{2,1,0:T(8,128)(2,1)S(1)} %collective-permute-done.7), channel_id=1, source_target_pairs={{0,448},{2,450},{4,452},{6,454},{8,456},{10,458},{12,460},{14,462}... | collective-permute-start | bytes 3145736 | tf_op jit(solution)/shard_map/ppermute | solution.py:130
  77.2 9.3 %collective-permute-start.11 = (bf16[2,64,2048]{2,1,0:T(8,128)(2,1)S(1)}, bf16[2,64,2048]{2,1,0:T(8,128)(2,1)S(1)}, u32[]{:S(2)}, u32[]{:S(2)}) collective-permute-start(bf16[2,64,2048]{2,1,0:T(8,128)(2,1)S(1)} %slice.66), channel_id=1, source_target_pairs={{1,449},{3,451},{5,453},{7,455},{9,457},{11,459},{13,461},{15,463}... | collective-permute-start | bytes 1572872 | tf_op jit(solution)/shard_map/ppermute | solution.py:134
  79.9 8.0 %collective-permute-start.10 = (bf16[2,64,2048]{2,1,0:T(8,128)(2,1)S(1)}, bf16[2,64,2048]{2,1,0:T(8,128)(2,1)S(1)}, u32[]{:S(2)}, u32[]{:S(2)}) collective-permute-start(bf16[2,64,2048]{2,1,0:T(8,128)(2,1)S(1)} %slice.65), channel_id=1, source_target_pairs={{1,65},{3,67},{5,69},{7,71},{9,73},{11,75},{13,77},{15,79},{17,81}... | collective-permute-start | bytes 1572872 | tf_op jit(solution)/shard_map/ppermute | solution.py:133

commit v3 on v2

--- a/solution.py
+++ b/solution.py
@@ -7,6 +7,7 @@
 
 GROUP = 128
 HALF = 128
+CHUNK = 2
 ADAPTER_GAIN = 0.5
 
 Z, X, YLO, YHI, CORE = 8, 4, 2, 4, 2
@@ -49,7 +50,7 @@
     return jnp.sum(jnp.where(rows == index, table, 0), axis=0, keepdims=True)
 
 
-def weight_kernel(words_ref, zero_ref, scale_ref, channel_ref, down_ref, up_ref, out_ref):
+def weight_kernel(words_ref, zero_ref, scale_ref, channel_ref, down_ref, up_ref, out_ref, *chunk_refs):
     group = pl.program_id(0)
     square = (GROUP, GROUP)
     diagonal = lax.broadcasted_iota(jnp.int32, square, 0) == lax.broadcasted_iota(jnp.int32, square, 1)
@@ -69,6 +70,11 @@
             out_ref[:, columns] = (
                 weight.astype(jnp.float32) * inverse + ADAPTER_GAIN * adapter
             ).astype(jnp.bfloat16)
+    for index, chunk_ref in enumerate(chunk_refs):
+
+        @pl.when(group // CHUNK == index)
+        def _(chunk_ref=chunk_ref):
+            chunk_ref[...] = out_ref[...]
 
 
 def effective_weight(words, zeros, scales, channel, down, up):
@@ -87,9 +93,14 @@
             pl.BlockSpec((rank, GROUP), lambda g: (0, g)),
             pl.BlockSpec((rank, cols), lambda g: (0, 0)),
         ],
-        out_specs=pl.BlockSpec((GROUP, cols), lambda g: (g, 0)),
-        out_shape=jax.ShapeDtypeStruct((rows, cols), jnp.bfloat16),
-        compiler_params=pltpu.CompilerParams(vmem_limit_bytes=8 * 1024 * 1024),
+        out_specs=[pl.BlockSpec((GROUP, cols), lambda g: (g, 0))]
+        + [
+            pl.BlockSpec((GROUP, cols), lambda g, i=i: (jnp.clip(g - CHUNK * i, 0, CHUNK - 1), 0))
+            for i in range(groups // CHUNK)
+        ],
+        out_shape=[jax.ShapeDtypeStruct((rows, cols), jnp.bfloat16)]
+        + [jax.ShapeDtypeStruct((CHUNK * GROUP, cols), jnp.bfloat16)] * (groups // CHUNK),
+        compiler_params=pltpu.CompilerParams(vmem_limit_bytes=12 * 1024 * 1024),
         cost_estimate=pl.CostEstimate(
             flops=12 * rows * cols, bytes_accessed=4 * rows * half_cols + 2 * rows * cols, transcendentals=0
         ),
@@ -120,9 +131,9 @@
     own = send_all(grad, PLANES).reshape(tokens, cols)
     own = jnp.stack([own, lax.ppermute(own, BOTH, TO_HOME)])
 
-    weight = effective_weight(words, zeros, scales, channel + 0 * own[1, 0, :k].astype(jnp.float32), down, up)
+    weight, *chunks = effective_weight(words, zeros, scales, channel + 0 * own[1, 0, :k].astype(jnp.float32), down, up)
     other_weight = jnp.concatenate(
-        [lax.ppermute(weight[i : i + 256], "narrow", OTHER_CORE) for i in range(0, k, 256)], 0
+        [lax.ppermute(chunk, "narrow", OTHER_CORE) for chunk in chunks], 0
     )
     low, high = [own], [own]
     for step in range(3):

time: 119 us -> 119 us (level)
  Pallas kernels: 3.07 us -> 5.15 us
  local copies, waits for them, and re-layouts: 6.86 us -> 5.07 us
    pallas_call x1, Pallas kernels: 3.07 us -> 5.15 us  [effective_weight(): pl.pallas_call(weight_kernel, grid=(groups,), in_specs=[pl.BlockSpec((GRO...]
    slice x1 -> x0, local copies, waits for them, and re-layouts: 1.79 us -> none  [shards(): weight[i:i + 256]]
  transfers between devices with their start and end apart: 12 -> 12, of which waited for: 6 -> 6; matrix products, arithmetic and copies ran while one was open for 11% -> 10% of each run, Pallas kernels for 3% -> 4%
where the time goes in v3:
time: 119 us
  blocking collectives  42.1 us (35%)
  starting transfers between devices  30.3 us (25%)
  waiting for transfers between devices  23.5 us (20%)
  matrix products  6.94 us (6%)
  other arithmetic  5.32 us (4%)
  Pallas kernels  5.15 us (4%)
  local copies, waits for them, and re-layouts  5.07 us (4%)
    all_to_all x1, blocking collectives, shards(): parts = lax.all_to_all(parts, BOTH, 0, 0, axis_index_groups=OWNERS)  26.8 us
    all_to_all x1, blocking collectives, send_all(): return lax.all_to_all(copies, 'wide', 0, 0, axis_index_groups=groups)  15.2 us
    ppermute x3, waiting for transfers between devices, shards(): high.append(lax.ppermute(high[-1], BOTH, hop(-1, step % 2 == 0)))  15 us
    ppermute x3, starting transfers between devices, shards(): lax.ppermute(chunk, 'narrow', OTHER_CORE)  12 us
    ppermute x3, starting transfers between devices, shards(): high.append(lax.ppermute(high[-1], BOTH, hop(-1, step % 2 == 0)))  6.84 us
    ppermute x3, starting transfers between devices, shards(): low.append(lax.ppermute(low[-1], BOTH, hop(1, step % 2 == 0)))  6.2 us
    pallas_call x1, Pallas kernels, effective_weight(): pl.pallas_call(weight_kernel, grid=(groups,), in_specs=[pl.BlockSpec((GRO...  5.15 us
    dot_general x3, matrix products, times(): lax.dot_general(block[0], weight, dims, preferred_element_type=jnp.float32)  3.49 us
  transfers between devices with their start and end apart: 12, of which 6 were waited for; matrix products, arithmetic and copies ran while one was open for 10% of the time, Pallas kernels for 4%

profile of v3, /device:TPU:64, one launch (start us, length us, event | category | flops | bytes accessed | tf_op | source)
XLA Modules:
  0.0 118.8 jit_solution(12157737874575249203)
XLA Ops:
  0.0 0.0 copy-start.9
  0.0 0.0 copy-start
  0.0 0.0 copy-start.1
  0.0 0.0 copy-start.2
  0.0 0.0 copy-start.4
  0.0 0.0 copy-start.3
  0.0 1.0 broadcast_in_dim.2
  1.1 15.2 %all_to_all.10 = bf16[8,16,2048]{2,1,0:T(8,128)(2,1)S(1)} all-to-all(bf16[8,16,2048]{2,1,0:T(8,128)(2,1)S(1)} %broadcast_in_dim.2), channel_id=1, replica_groups={{0,8,16,24,32,40,48,56},{64,72,80,88,96,104,112,120},{128,136,144,152,1..., dimensions={0} | all-to-all | bytes 1048576 | tf_op jit(solution)/shard_map/all_to_all | solution.py:112
  16.3 0.0 copy-start.5
  16.3 1.3 %collective-permute-start = (bf16[128,2048]{1,0:T(8,128)(2,1)S(1)}, bf16[128,2048]{1,0:T(8,128)(2,1)S(1)}, u32[]{:S(2)}, u32[]{:S(2)}) collective-permute-start(bf16[128,2048]{1,0:T(8,128)(2,1)S(1)} %bitcast.41), channel_id=1, source_target_pairs={{1,0},{3,2},{5,4},{7,6},{9,8},{11,10},{13,12},{15,14},{17,16},{19,... | collective-permute-start | bytes 1572872 | tf_op jit(solution)/shard_map/ppermute | solution.py:132
  17.6 1.5 %collective-permute-done = bf16[128,2048]{1,0:T(8,128)(2,1)S(1)} collective-permute-done((bf16[128,2048]{1,0:T(8,128)(2,1)S(1)}, bf16[128,2048]{1,0:T(8,128)(2,1)S(1)}, u32[]{:S(2)}, u32[]{:S(2)}) %collective-permute-start) | collective-permute-done | bytes 524320 | tf_op jit(solution)/shard_map/ppermute | solution.py:132
  19.1 0.0 copy-start.7
  19.1 1.2 pad_maximum_fusion.1
  20.3 1.3 %collective-permute-start.2 = (bf16[2,128,2048]{2,1,0:T(8,128)(2,1)}, bf16[2,128,2048]{2,1,0:T(8,128)(2,1)}, u32[]{:S(2)}, u32[]{:S(2)}) collective-permute-start(bf16[2,128,2048]{2,1,0:T(8,128)(2,1)} %pad_maximum_fusion.1), channel_id=1, source_target_pairs={{0,64},{2,66},{4,68},{6,70},{8,72},{10,74},{12,76},{14,78},{16,80}... | collective-permute-start | bytes 3145736 | tf_op jit(solution)/shard_map/ppermute | solution.py:140
  21.6 1.3 %collective-permute-start.1 = (bf16[2,128,2048]{2,1,0:T(8,128)(2,1)}, bf16[2,128,2048]{2,1,0:T(8,128)(2,1)}, u32[]{:S(2)}, u32[]{:S(2)}) collective-permute-start(bf16[2,128,2048]{2,1,0:T(8,128)(2,1)} %pad_maximum_fusion.1), channel_id=1, source_target_pairs={{0,448},{2,450},{4,452},{6,454},{8,456},{10,458},{12,460},{14,462}... | collective-permute-start | bytes 3145736 | tf_op jit(solution)/shard_map/ppermute | solution.py:141
  22.9 0.0 copy-done.9
  22.9 0.0 copy-done.5
  22.9 0.0 copy-done.7
  22.9 0.0 copy-done
  23.0 0.0 copy-done.1
  23.0 0.0 copy-done.2
  23.0 0.0 copy-done.4
  23.0 0.0 copy-done.3
  23.0 5.1 %shard_map.73 = (bf16[768,2048]{1,0:T(8,128)(2,1)S(1)}, bf16[256,2048]{1,0:T(8,128)(2,1)}, bf16[256,2048]{1,0:T(8,128)(2,1)}, bf16[256,2048]{1,0:T(8,128)(2,1)}) custom-call(s32[768,1024]{1,0:T(8,128)S(1)} %copy-done, s32[6,2048]{1,0:T(8,128)S(1)} %copy-done.1, f32[6,2048]{1,0:T(8,128)S(1)} %copy-done.2, f32[1,768]{1,0:T(1,128)S(1)} %reshape.11.channel_ref, ...), custom_call_target="tpu_custom_call" | custom-call | flops 18874368 | bytes 6291456 | tf_op jit(solution)/shard_map/pallas_call | solution.py:85
  28.1 7.7 %collective-permute-start.4 = (bf16[256,2048]{1,0:T(8,128)(2,1)}, bf16[256,2048]{1,0:T(8,128)(2,1)}, u32[]{:S(2)}, u32[]{:S(2)}) collective-permute-start(bf16[256,2048]{1,0:T(8,128)(2,1)} %get-tuple-element.10), channel_id=1, source_target_pairs={{0,1},{1,0},{2,3},{3,2},{4,5},{5,4},{6,7},{7,6},{8,9},{9,8},{10,11... | collective-permute-start | bytes 3145736 | tf_op jit(solution)/shard_map/ppermute | solution.py:136
  35.8 1.9 %collective-permute-start.5 = (bf16[256,2048]{1,0:T(8,128)(2,1)}, bf16[256,2048]{1,0:T(8,128)(2,1)}, u32[]{:S(2)}, u32[]{:S(2)}) collective-permute-start(bf16[256,2048]{1,0:T(8,128)(2,1)} %get-tuple-element.11), channel_id=1, source_target_pairs={{0,1},{1,0},{2,3},{3,2},{4,5},{5,4},{6,7},{7,6},{8,9},{9,8},{10,11... | collective-permute-start | bytes 3145736 | tf_op jit(solution)/shard_map/ppermute | solution.py:136
  37.7 2.4 %collective-permute-start.6 = (bf16[256,2048]{1,0:T(8,128)(2,1)}, bf16[256,2048]{1,0:T(8,128)(2,1)}, u32[]{:S(2)}, u32[]{:S(2)}) collective-permute-start(bf16[256,2048]{1,0:T(8,128)(2,1)} %get-tuple-element.12), channel_id=1, source_target_pairs={{0,1},{1,0},{2,3},{3,2},{4,5},{5,4},{6,7},{7,6},{8,9},{9,8},{10,11... | collective-permute-start | bytes 3145736 | tf_op jit(solution)/shard_map/ppermute | solution.py:136
  40.2 0.0 copy-start.6
  40.2 0.0 copy-start.8
  40.2 0.0 collective-permute-done.2
  40.2 3.6 %collective-permute-start.3 = (bf16[2,128,2048]{2,1,0:T(8,128)(2,1)}, bf16[2,128,2048]{2,1,0:T(8,128)(2,1)S(1)}, u32[]{:S(2)}, u32[]{:S(2)}) collective-permute-start(bf16[2,128,2048]{2,1,0:T(8,128)(2,1)} %collective-permute-done.2), channel_id=1, source_target_pairs={{1,65},{3,67},{5,69},{7,71},{9,73},{11,75},{13,77},{15,79},{17,81}... | collective-permute-start | bytes 3145736 | tf_op jit(solution)/shard_map/ppermute | solution.py:140
  43.9 0.0 collective-permute-done.1
  43.9 4.3 %collective-permute-start.7 = (bf16[2,128,2048]{2,1,0:T(8,128)(2,1)}, bf16[2,128,2048]{2,1,0:T(8,128)(2,1)S(1)}, u32[]{:S(2)}, u32[]{:S(2)}) collective-permute-start(bf16[2,128,2048]{2,1,0:T(8,128)(2,1)} %collective-permute-done.1), channel_id=1, source_target_pairs={{1,449},{3,451},{5,453},{7,455},{9,457},{11,459},{13,461},{15,463}... | collective-permute-start | bytes 3145736 | tf_op jit(solution)/shard_map/ppermute | solution.py:141
  48.1 0.0 collective-permute-done.4
  48.2 1.3 %constant_dynamic-update-slice_fusion.2 = bf16[768,2048]{1,0:T(8,128)(2,1)S(1)} fusion(bf16[256,2048]{1,0:T(8,128)(2,1)} %collective-permute-done.4), kind=kLoop, calls=%fused_computation.33 | loop fusion | bytes 2097152
  49.5 0.0 collective-permute-done.5
  49.5 1.3 %constant_dynamic-update-slice_fusion.1 = bf16[768,2048]{1,0:T(8,128)(2,1)S(1)} fusion(bf16[768,2048]{1,0:T(8,128)(2,1)S(1)} %constant_dynamic-update-slice_fusion.2, bf16[256,2048]{1,0:T(8,128)(2,1)} %collective-permute-done.5), kind=kLoop, calls=%fused_computation.32 | loop fusion | bytes 2097152
  50.8 0.0 collective-permute-done.6
  50.8 1.3 %constant_dynamic-update-slice_fusion = bf16[768,2048]{1,0:T(8,128)(2,1)S(1)} fusion(bf16[768,2048]{1,0:T(8,128)(2,1)S(1)} %constant_dynamic-update-slice_fusion.1, bf16[256,2048]{1,0:T(8,128)(2,1)} %collective-permute-done.6), kind=kLoop, calls=%fused_computation.31 | loop fusion | bytes 2097152 | tf_op jit(solution)/shard_map/concatenate | solution.py:135
  52.1 0.0 copy-done.6
  52.1 0.0 copy-done.8
  52.1 1.4 %broadcast_select_fusion.2 = bf16[2,128,2048]{2,1,0:T(8,128)(2,1)S(1)} fusion(bf16[2,128,2048]{2,1,0:T(8,128)(2,1)} %collective-permute-done.1, pred[]{:T(512)S(6)} %eq.3, bf16[1,128,2048]{2,1,0:T(8,128)(2,1)S(1)} %bitcast.46, bf16[1,128,2048]{2,1,0:T(8,128)(2,1)S(1)} %bitcast.43), kind=kLoop, calls=%fused_computation.21 | loop fusion | flops 1048576 | bytes 3145729 | tf_op jit(solution)/shard_map/jit(_where)/select_n | solution.py:150
  53.5 2.9 %collective-permute-done.3 = bf16[2,128,2048]{2,1,0:T(8,128)(2,1)S(1)} collective-permute-done((bf16[2,128,2048]{2,1,0:T(8,128)(2,1)}, bf16[2,128,2048]{2,1,0:T(8,128)(2,1)S(1)}, u32[]{:S(2)}, u32[]{:S(2)}) %collective-permute-start.3) | collective-permute-done | bytes 1048608 | tf_op jit(solution)/shard_map/ppermute | solution.py:140
  56.4 1.3 %collective-permute-start.9 = (bf16[2,128,2048]{2,1,0:T(8,128)(2,1)S(1)}, bf16[2,128,2048]{2,1,0:T(8,128)(2,1)S(1)}, u32[]{:S(2)}, u32[]{:S(2)}) collective-permute-start(bf16[2,128,2048]{2,1,0:T(8,128)(2,1)S(1)} %collective-permute-done.3), channel_id=1, source_target_pairs={{0,64},{2,66},{4,68},{6,70},{8,72},{10,74},{12,76},{14,78},{16,80}... | collective-permute-start | bytes 3145736 | tf_op jit(solution)/shard_map/ppermute | solution.py:140
  57.7 3.0 %collective-permute-done.7 = bf16[2,128,2048]{2,1,0:T(8,128)(2,1)S(1)} collective-permute-done((bf16[2,128,2048]{2,1,0:T(8,128)(2,1)}, bf16[2,128,2048]{2,1,0:T(8,128)(2,1)S(1)}, u32[]{:S(2)}, u32[]{:S(2)}) %collective-permute-start.7) | collective-permute-done | bytes 1048608 | tf_op jit(solution)/shard_map/ppermute | solution.py:141
  60.7 1.3 %collective-permute-start.8 = (bf16[2,128,2048]{2,1,0:T(8,128)(2,1)S(1)}, bf16[2,128,2048]{2,1,0:T(8,128)(2,1)S(1)}, u32[]{:S(2)}, u32[]{:S(2)}) collective-permute-start(bf16[2,128,2048]{2,1,0:T(8,128)(2,1)S(1)} %collective-permute-done.7), channel_id=1, source_target_pairs={{0,448},{2,450},{4,452},{6,454},{8,456},{10,458},{12,460},{14,462}... | collective-permute-start | bytes 3145736 | tf_op jit(solution)/shard_map/ppermute | solution.py:141
  62.0 1.3 %broadcast_select_fusion.1 = bf16[2,128,2048]{2,1,0:T(8,128)(2,1)S(1)} fusion(bf16[2,128,2048]{2,1,0:T(8,128)(2,1)S(1)} %collective-permute-done.3, bf16[2,128,2048]{2,1,0:T(8,128)(2,1)} %collective-permute-done.2, pred[]{:T(512)S(6)} %eq.3), kind=kLoop, calls=%fused_computation.20 | loop fusion | flops 524288 | bytes 3145729 | tf_op jit(solution)/shard_map/jit(_where)/select_n | solution.py:153
  63.3 1.0 fusion.15
  64.4 1.1 fusion.11
  65.5 12.0 %collective-permute-done.8 = bf16[2,128,2048]{2,1,0:T(8,128)(2,1)S(1)} collective-permute-done((bf16[2,128,2048]{2,1,0:T(8,128)(2,1)S(1)}, bf16[2,128,2048]{2,1,0:T(8,128)(2,1)S(1)}, u32[]{:S(2)}, u32[]{:S(2)}) %collective-permute-start.8) | collective-permute-done | bytes 1048608 | tf_op jit(solution)/shard_map/ppermute | solution.py:141
  77.6 2.6 %collective-permute-start.11 = (bf16[2,64,2048]{2,1,0:T(8,128)(2,1)S(1)}, bf16[2,64,2048]{2,1,0:T(8,128)(2,1)S(1)}, u32[]{:S(2)}, u32[]{:S(2)}) collective-permute-start(bf16[2,64,2048]{2,1,0:T(8,128)(2,1)S(1)} %slice.51), channel_id=1, source_target_pairs={{1,449},{3,451},{5,453},{7,455},{9,457},{11,459},{13,461},{15,463}... | collective-permute-start | bytes 1572872 | tf_op jit(solution)/shard_map/ppermute | solution.py:145
  80.2 0.0 collective-permute-done.9
  80.2 1.3 %collective-permute-start.10 = (bf16[2,64,2048]{2,1,0:T(8,128)(2,1)S(1)}, bf16[2,64,2048]{2,1,0:T(8,128)(2,1)S(1)}, u32[]{:S(2)}, u32[]{:S(2)}) collective-permute-start(bf16[2,64,2048]{2,1,0:T(8,128)(2,1)S(1)} %slice.50), channel_id=1, source_target_pairs={{1,65},{3,67},{5,69},{7,71},{9,73},{11,75},{13,77},{15,79},{17,81}... | collective-permute-start | bytes 1572872 | tf_op jit(solution)/shard_map/ppermute | solution.py:144
  81.6 0.1 broadcast_select_fusion
  81.7 1.2 %fusion.19 = f32[128,768]{1,0:T(8,128)S(1)} fusion(bf16[768,2048]{1,0:T(8,128)(2,1)S(1)} %constant_dynamic-update-slice_fusion, bf16[2,128,2048]{2,1,0:T(8,128)(2,1)S(1)} %broadcast_select_fusion), kind=kOutput, calls=%fused_computation.27 | convolution fusion | flops 402653184 | bytes 4063232 | tf_op jit(solution)/shard_map/dot_general | solution.py:117
  82.9 1.2 fusion.3
  84.1 2.7 %collective-permute-done.11 = bf16[2,64,2048]{2,1,0:T(8,128)(2,1)S(1)} collective-permute-done((bf16[2,64,2048]{2,1,0:T(8,128)(2,1)S(1)}, bf16[2,64,2048]{2,1,0:T(8,128)(2,1)S(1)}, u32[]{:S(2)}, u32[]{:S(2)}) %collective-permute-start.11) | collective-permute-done | bytes 524320 | tf_op jit(solution)/shard_map/ppermute | solution.py:145
  86.8 1.4 %collective-permute-done.10 = bf16[2,64,2048]{2,1,0:T(8,128)(2,1)S(1)} collective-permute-done((bf16[2,64,2048]{2,1,0:T(8,128)(2,1)S(1)}, bf16[2,64,2048]{2,1,0:T(8,128)(2,1)S(1)}, u32[]{:S(2)}, u32[]{:S(2)}) %collective-permute-start.10) | collective-permute-done | bytes 524320 | tf_op jit(solution)/shard_map/ppermute | solution.py:144
  88.2 0.4 maximum_select_fusion
  88.6 1.2 %fusion.18 = f32[128,768]{1,0:T(8,128)S(1)} fusion(bf16[768,2048]{1,0:T(8,128)(2,1)S(1)} %constant_dynamic-update-slice_fusion, bf16[2,128,2048]{2,1,0:T(8,128)(2,1)S(1)} %maximum_select_fusion), kind=kOutput, calls=%fused_computation.24 | convolution fusion | flops 402653184 | bytes 4063232 | tf_op jit(solution)/shard_map/dot_general | solution.py:117
  89.8 1.2 fusion.2
  91.0 0.1 pad_maximum_fusion.2
  91.1 26.8 %all_to_all.11 = bf16[4,128,768]{2,1,0:T(8,128)(2,1)S(1)} all-to-all(bf16[4,128,768]{2,1,0:T(8,128)(2,1)S(1)} %pad_maximum_fusion.2), channel_id=1, replica_groups={{0,2,4,6},{1,3,5,7},{8,10,12,14},{9,11,13,15},{16,18,20,22},{17,19,21,2..., dimensions={0} | all-to-all | bytes 1572864 | tf_op jit(solution)/shard_map/all_to_all | solution.py:160
  118.0 0.8 reduce_sum.12
  (6 shorter events, 0.1 us)
Async XLA Ops:
  0.0 22.9 %copy-start.9 = (f32[768]{0:T(1024)S(1)}, f32[768]{0:T(1024)}, u32[]{:S(2)}) copy-start(f32[768]{0:T(1024)} %param.11) | copy-start | bytes 9220
  0.0 22.9 %copy-start = (s32[768,1024]{1,0:T(8,128)S(1)}, s32[768,1024]{1,0:T(8,128)}, u32[]{:S(2)}) copy-start(s32[768,1024]{1,0:T(8,128)} %words_ref.1) | copy-start | bytes 9437188
  0.0 22.9 %copy-start.1 = (s32[6,2048]{1,0:T(8,128)S(1)}, s32[6,2048]{1,0:T(8,128)}, u32[]{:S(2)}) copy-start(s32[6,2048]{1,0:T(8,128)} %zero_ref.1) | copy-start | bytes 147460
  0.0 23.0 %copy-start.2 = (f32[6,2048]{1,0:T(8,128)S(1)}, f32[6,2048]{1,0:T(8,128)}, u32[]{:S(2)}) copy-start(f32[6,2048]{1,0:T(8,128)} %scale_ref.1) | copy-start | bytes 147460
  0.0 23.0 %copy-start.4 = (bf16[768,16]{0,1:T(8,128)(2,1)S(1)}, bf16[768,16]{0,1:T(8,128)(2,1)}, u32[]{:S(2)}) copy-start(bf16[768,16]{0,1:T(8,128)(2,1)} %param.12) | copy-start | bytes 73732
  0.0 23.0 %copy-start.3 = (bf16[16,2048]{1,0:T(8,128)(2,1)S(1)}, bf16[16,2048]{1,0:T(8,128)(2,1)}, u32[]{:S(2)}) copy-start(bf16[16,2048]{1,0:T(8,128)(2,1)} %up_ref.1) | copy-start | bytes 196612
  16.3 6.6 %copy-start.5 = (bf16[8,16,2048]{2,1,0:T(8,128)(2,1)}, bf16[8,16,2048]{2,1,0:T(8,128)(2,1)S(1)}, u32[]{:S(2)}) copy-start(bf16[8,16,2048]{2,1,0:T(8,128)(2,1)S(1)} %all_to_all.10) | copy-start | bytes 1572868
  16.3 2.8 %collective-permute-start = (bf16[128,2048]{1,0:T(8,128)(2,1)S(1)}, bf16[128,2048]{1,0:T(8,128)(2,1)S(1)}, u32[]{:S(2)}, u32[]{:S(2)}) collective-permute-start(bf16[128,2048]{1,0:T(8,128)(2,1)S(1)} %bitcast.41), channel_id=1, source_target_pairs={{1,0},{3,2},{5,4},{7,6},{9,8},{11,10},{13,12},{15,14},{17,16},{19,... | collective-permute-start | bytes 1572872 | tf_op jit(solution)/shard_map/ppermute | solution.py:132
  19.1 3.8 %copy-start.7 = (bf16[128,2048]{1,0:T(8,128)(2,1)}, bf16[128,2048]{1,0:T(8,128)(2,1)S(1)}, u32[]{:S(2)}) copy-start(bf16[128,2048]{1,0:T(8,128)(2,1)S(1)} %collective-permute-done) | copy-start | bytes 1572868
  20.3 19.9 %collective-permute-start.2 = (bf16[2,128,2048]{2,1,0:T(8,128)(2,1)}, bf16[2,128,2048]{2,1,0:T(8,128)(2,1)}, u32[]{:S(2)}, u32[]{:S(2)}) collective-permute-start(bf16[2,128,2048]{2,1,0:T(8,128)(2,1)} %pad_maximum_fusion.1), channel_id=1, source_target_pairs={{0,64},{2,66},{4,68},{6,70},{8,72},{10,74},{12,76},{14,78},{16,80}... | collective-permute-start | bytes 3145736 | tf_op jit(solution)/shard_map/ppermute | solution.py:140
  21.6 22.3 %collective-permute-start.1 = (bf16[2,128,2048]{2,1,0:T(8,128)(2,1)}, bf16[2,128,2048]{2,1,0:T(8,128)(2,1)}, u32[]{:S(2)}, u32[]{:S(2)}) collective-permute-start(bf16[2,128,2048]{2,1,0:T(8,128)(2,1)} %pad_maximum_fusion.1), channel_id=1, source_target_pairs={{0,448},{2,450},{4,452},{6,454},{8,456},{10,458},{12,460},{14,462}... | collective-permute-start | bytes 3145736 | tf_op jit(solution)/shard_map/ppermute | solution.py:141
  28.1 20.0 %collective-permute-start.4 = (bf16[256,2048]{1,0:T(8,128)(2,1)}, bf16[256,2048]{1,0:T(8,128)(2,1)}, u32[]{:S(2)}, u32[]{:S(2)}) collective-permute-start(bf16[256,2048]{1,0:T(8,128)(2,1)} %get-tuple-element.10), channel_id=1, source_target_pairs={{0,1},{1,0},{2,3},{3,2},{4,5},{5,4},{6,7},{7,6},{8,9},{9,8},{10,11... | collective-permute-start | bytes 3145736 | tf_op jit(solution)/shard_map/ppermute | solution.py:136
  35.8 13.6 %collective-permute-start.5 = (bf16[256,2048]{1,0:T(8,128)(2,1)}, bf16[256,2048]{1,0:T(8,128)(2,1)}, u32[]{:S(2)}, u32[]{:S(2)}) collective-permute-start(bf16[256,2048]{1,0:T(8,128)(2,1)} %get-tuple-element.11), channel_id=1, source_target_pairs={{0,1},{1,0},{2,3},{3,2},{4,5},{5,4},{6,7},{7,6},{8,9},{9,8},{10,11... | collective-permute-start | bytes 3145736 | tf_op jit(solution)/shard_map/ppermute | solution.py:136
  37.7 13.0 %collective-permute-start.6 = (bf16[256,2048]{1,0:T(8,128)(2,1)}, bf16[256,2048]{1,0:T(8,128)(2,1)}, u32[]{:S(2)}, u32[]{:S(2)}) collective-permute-start(bf16[256,2048]{1,0:T(8,128)(2,1)} %get-tuple-element.12), channel_id=1, source_target_pairs={{0,1},{1,0},{2,3},{3,2},{4,5},{5,4},{6,7},{7,6},{8,9},{9,8},{10,11... | collective-permute-start | bytes 3145736 | tf_op jit(solution)/shard_map/ppermute | solution.py:136
  40.2 11.9 %copy-start.6 = (bf16[8,16,2048]{2,1,0:T(8,128)(2,1)S(1)}, bf16[8,16,2048]{2,1,0:T(8,128)(2,1)}, u32[]{:S(2)}) copy-start(bf16[8,16,2048]{2,1,0:T(8,128)(2,1)} %copy-done.5) | copy-start | bytes 1572868
  40.2 11.9 %copy-start.8 = (bf16[128,2048]{1,0:T(8,128)(2,1)S(1)}, bf16[128,2048]{1,0:T(8,128)(2,1)}, u32[]{:S(2)}) copy-start(bf16[128,2048]{1,0:T(8,128)(2,1)} %copy-done.7) | copy-start | bytes 1572868
  40.2 16.2 %collective-permute-start.3 = (bf16[2,128,2048]{2,1,0:T(8,128)(2,1)}, bf16[2,128,2048]{2,1,0:T(8,128)(2,1)S(1)}, u32[]{:S(2)}, u32[]{:S(2)}) collective-permute-start(bf16[2,128,2048]{2,1,0:T(8,128)(2,1)} %collective-permute-done.2), channel_id=1, source_target_pairs={{1,65},{3,67},{5,69},{7,71},{9,73},{11,75},{13,77},{15,79},{17,81}... | collective-permute-start | bytes 3145736 | tf_op jit(solution)/shard_map/ppermute | solution.py:140
  43.9 16.8 %collective-permute-start.7 = (bf16[2,128,2048]{2,1,0:T(8,128)(2,1)}, bf16[2,128,2048]{2,1,0:T(8,128)(2,1)S(1)}, u32[]{:S(2)}, u32[]{:S(2)}) collective-permute-start(bf16[2,128,2048]{2,1,0:T(8,128)(2,1)} %collective-permute-done.1), channel_id=1, source_target_pairs={{1,449},{3,451},{5,453},{7,455},{9,457},{11,459},{13,461},{15,463}... | collective-permute-start | bytes 3145736 | tf_op jit(solution)/shard_map/ppermute | solution.py:141
  56.4 23.8 %collective-permute-start.9 = (bf16[2,128,2048]{2,1,0:T(8,128)(2,1)S(1)}, bf16[2,128,2048]{2,1,0:T(8,128)(2,1)S(1)}, u32[]{:S(2)}, u32[]{:S(2)}) collective-permute-start(bf16[2,128,2048]{2,1,0:T(8,128)(2,1)S(1)} %collective-permute-done.3), channel_id=1, source_target_pairs={{0,64},{2,66},{4,68},{6,70},{8,72},{10,74},{12,76},{14,78},{16,80}... | collective-permute-start | bytes 3145736 | tf_op jit(solution)/shard_map/ppermute | solution.py:140
  60.7 16.8 %collective-permute-start.8 = (bf16[2,128,2048]{2,1,0:T(8,128)(2,1)S(1)}, bf16[2,128,2048]{2,1,0:T(8,128)(2,1)S(1)}, u32[]{:S(2)}, u32[]{:S(2)}) collective-permute-start(bf16[2,128,2048]{2,1,0:T(8,128)(2,1)S(1)} %collective-permute-done.7), channel_id=1, source_target_pairs={{0,448},{2,450},{4,452},{6,454},{8,456},{10,458},{12,460},{14,462}... | collective-permute-start | bytes 3145736 | tf_op jit(solution)/shard_map/ppermute | solution.py:141
  77.6 9.3 %collective-permute-start.11 = (bf16[2,64,2048]{2,1,0:T(8,128)(2,1)S(1)}, bf16[2,64,2048]{2,1,0:T(8,128)(2,1)S(1)}, u32[]{:S(2)}, u32[]{:S(2)}) collective-permute-start(bf16[2,64,2048]{2,1,0:T(8,128)(2,1)S(1)} %slice.51), channel_id=1, source_target_pairs={{1,449},{3,451},{5,453},{7,455},{9,457},{11,459},{13,461},{15,463}... | collective-permute-start | bytes 1572872 | tf_op jit(solution)/shard_map/ppermute | solution.py:145
  80.2 8.0 %collective-permute-start.10 = (bf16[2,64,2048]{2,1,0:T(8,128)(2,1)S(1)}, bf16[2,64,2048]{2,1,0:T(8,128)(2,1)S(1)}, u32[]{:S(2)}, u32[]{:S(2)}) collective-permute-start(bf16[2,64,2048]{2,1,0:T(8,128)(2,1)S(1)} %slice.50), channel_id=1, source_target_pairs={{1,65},{3,67},{5,69},{7,71},{9,73},{11,75},{13,77},{15,79},{17,81}... | collective-permute-start | bytes 1572872 | tf_op jit(solution)/shard_map/ppermute | solution.py:144

commit v4 on v3

--- a/solution.py
+++ b/solution.py
@@ -152,11 +152,11 @@
         jnp.where(home, far, low[3]),
         jnp.where(home, low[2], low[1]),
     ]
-    blocks[1:3] = [lax.optimization_barrier(block) for block in blocks[1:3]]
-    pair = jnp.concatenate([blocks[0], blocks[3]], 1)
-    pair = times(pair, weight, other_weight).astype(jnp.bfloat16)
-    middle = [times(block, weight, other_weight).astype(jnp.bfloat16) for block in blocks[1:3]]
-    parts = jnp.stack([pair[:tokens], *middle, pair[tokens:]])
+    early, late = [
+        times(jnp.concatenate([blocks[i], blocks[j]], 1), weight, other_weight).astype(jnp.bfloat16)
+        for i, j in ((0, 3), (1, 2))
+    ]
+    parts = jnp.stack([early[:tokens], late[:tokens], late[tokens:], early[tokens:]])
     parts = lax.all_to_all(parts, BOTH, 0, 0, axis_index_groups=OWNERS)
     return jnp.sum(parts.astype(jnp.float32), axis=0).astype(jnp.bfloat16)
 

time: 119 us -> 118 us (level)
  matrix products: 6.94 us -> 4.31 us
  waiting for transfers between devices: 23.5 us -> 25.5 us
    ppermute x3, waiting for transfers between devices: 15 us -> 3.01 us  [shards(): high.append(lax.ppermute(high[-1], BOTH, hop(-1, step % 2 == 0)))]
    ppermute x3, waiting for transfers between devices: 2.94 us -> 14.4 us  [shards(): low.append(lax.ppermute(low[-1], BOTH, hop(1, step % 2 == 0)))]
    ppermute x1, waiting for transfers between devices: 1.39 us -> 4.73 us  [shards(): lax.ppermute(low[3][:, :mid], BOTH, hop(1, False))]
    dot_general x3 -> x2, matrix products: 3.45 us -> 2.03 us  [times(): lax.dot_general(block[1], other_weight, dims, preferred_element_type=jnp....]
    dot_general x3 -> x2, matrix products: 3.49 us -> 2.28 us  [times(): lax.dot_general(block[0], weight, dims, preferred_element_type=jnp.float32)]
  transfers between devices with their start and end apart: 12 -> 12, of which waited for: 6 -> 6; matrix products, arithmetic and copies ran while one was open for 10% -> 8% of each run, Pallas kernels for 4% -> 4%
where the time goes in v4:
time: 118 us; the launch traced here: 117 us
  blocking collectives  42.3 us (36%)
  starting transfers between devices  29.4 us (25%)
  waiting for transfers between devices  25.5 us (22%)
  other arithmetic  5.31 us (4%)
  Pallas kernels  5.15 us (4%)
  local copies, waits for them, and re-layouts  5.09 us (4%)
  matrix products  4.31 us (4%)
    all_to_all x1, blocking collectives, shards(): parts = lax.all_to_all(parts, BOTH, 0, 0, axis_index_groups=OWNERS)  26.9 us
    all_to_all x1, blocking collectives, send_all(): return lax.all_to_all(copies, 'wide', 0, 0, axis_index_groups=groups)  15.4 us
    ppermute x3, waiting for transfers between devices, shards(): low.append(lax.ppermute(low[-1], BOTH, hop(1, step % 2 == 0)))  14.4 us
    ppermute x3, starting transfers between devices, shards(): lax.ppermute(chunk, 'narrow', OTHER_CORE)  12 us
    ppermute x3, starting transfers between devices, shards(): high.append(lax.ppermute(high[-1], BOTH, hop(-1, step % 2 == 0)))  6.84 us
    ppermute x3, starting transfers between devices, shards(): low.append(lax.ppermute(low[-1], BOTH, hop(1, step % 2 == 0)))  6.2 us
    pallas_call x1, Pallas kernels, effective_weight(): pl.pallas_call(weight_kernel, grid=(groups,), in_specs=[pl.BlockSpec((GRO...  5.15 us
    ppermute x1, waiting for transfers between devices, shards(): lax.ppermute(low[3][:, :mid], BOTH, hop(1, False))  4.73 us
  transfers between devices with their start and end apart: 12, of which 6 were waited for; matrix products, arithmetic and copies ran while one was open for 8% of the time, Pallas kernels for 4%

profile of v4, /device:TPU:64, one launch (start us, length us, event | category | flops | bytes accessed | tf_op | source)
XLA Modules:
  0.0 117.4 jit_solution(12253390017477262678)
XLA Ops:
  0.0 0.0 copy-start.9
  0.0 0.0 copy-start.3
  0.0 0.0 copy-start.4
  0.0 0.0 copy-start.2
  0.0 0.0 copy-start.1
  0.0 0.0 copy-start
  0.0 1.0 broadcast_in_dim.2
  1.1 15.4 %all_to_all.10 = bf16[8,16,2048]{2,1,0:T(8,128)(2,1)S(1)} all-to-all(bf16[8,16,2048]{2,1,0:T(8,128)(2,1)S(1)} %broadcast_in_dim.2), channel_id=1, replica_groups={{0,8,16,24,32,40,48,56},{64,72,80,88,96,104,112,120},{128,136,144,152,1..., dimensions={0} | all-to-all | bytes 1048576 | tf_op jit(solution)/shard_map/all_to_all | solution.py:112
  16.4 0.0 copy-start.5
  16.4 1.3 %collective-permute-start = (bf16[128,2048]{1,0:T(8,128)(2,1)S(1)}, bf16[128,2048]{1,0:T(8,128)(2,1)S(1)}, u32[]{:S(2)}, u32[]{:S(2)}) collective-permute-start(bf16[128,2048]{1,0:T(8,128)(2,1)S(1)} %bitcast.37), channel_id=1, source_target_pairs={{1,0},{3,2},{5,4},{7,6},{9,8},{11,10},{13,12},{15,14},{17,16},{19,... | collective-permute-start | bytes 1572872 | tf_op jit(solution)/shard_map/ppermute | solution.py:132
  17.8 1.5 %collective-permute-done = bf16[128,2048]{1,0:T(8,128)(2,1)S(1)} collective-permute-done((bf16[128,2048]{1,0:T(8,128)(2,1)S(1)}, bf16[128,2048]{1,0:T(8,128)(2,1)S(1)}, u32[]{:S(2)}, u32[]{:S(2)}) %collective-permute-start) | collective-permute-done | bytes 524320 | tf_op jit(solution)/shard_map/ppermute | solution.py:132
  19.3 0.0 copy-start.7
  19.3 1.2 pad_maximum_fusion.2
  20.4 1.3 %collective-permute-start.2 = (bf16[2,128,2048]{2,1,0:T(8,128)(2,1)}, bf16[2,128,2048]{2,1,0:T(8,128)(2,1)}, u32[]{:S(2)}, u32[]{:S(2)}) collective-permute-start(bf16[2,128,2048]{2,1,0:T(8,128)(2,1)} %pad_maximum_fusion.2), channel_id=1, source_target_pairs={{0,64},{2,66},{4,68},{6,70},{8,72},{10,74},{12,76},{14,78},{16,80}... | collective-permute-start | bytes 3145736 | tf_op jit(solution)/shard_map/ppermute | solution.py:140
  21.7 1.3 %collective-permute-start.1 = (bf16[2,128,2048]{2,1,0:T(8,128)(2,1)}, bf16[2,128,2048]{2,1,0:T(8,128)(2,1)}, u32[]{:S(2)}, u32[]{:S(2)}) collective-permute-start(bf16[2,128,2048]{2,1,0:T(8,128)(2,1)} %pad_maximum_fusion.2), channel_id=1, source_target_pairs={{0,448},{2,450},{4,452},{6,454},{8,456},{10,458},{12,460},{14,462}... | collective-permute-start | bytes 3145736 | tf_op jit(solution)/shard_map/ppermute | solution.py:141
  23.0 0.0 copy-done.9
  23.1 0.0 copy-done.3
  23.1 0.0 copy-done.4
  23.1 0.0 copy-done.2
  23.1 0.0 copy-done.1
  23.1 0.0 copy-done
  23.1 5.1 %shard_map.73 = (bf16[768,2048]{1,0:T(8,128)(2,1)S(1)}, bf16[256,2048]{1,0:T(8,128)(2,1)}, bf16[256,2048]{1,0:T(8,128)(2,1)}, bf16[256,2048]{1,0:T(8,128)(2,1)}) custom-call(s32[768,1024]{1,0:T(8,128)S(1)} %copy-done, s32[6,2048]{1,0:T(8,128)S(1)} %copy-done.1, f32[6,2048]{1,0:T(8,128)S(1)} %copy-done.2, f32[1,768]{1,0:T(1,128)S(1)} %reshape.11.channel_ref, ...), custom_call_target="tpu_custom_call" | custom-call | flops 18874368 | bytes 6291456 | tf_op jit(solution)/shard_map/pallas_call | solution.py:85
  28.3 0.0 copy-done.5
  28.3 0.0 copy-done.7
  28.3 7.7 %collective-permute-start.4 = (bf16[256,2048]{1,0:T(8,128)(2,1)}, bf16[256,2048]{1,0:T(8,128)(2,1)}, u32[]{:S(2)}, u32[]{:S(2)}) collective-permute-start(bf16[256,2048]{1,0:T(8,128)(2,1)} %get-tuple-element.10), channel_id=1, source_target_pairs={{0,1},{1,0},{2,3},{3,2},{4,5},{5,4},{6,7},{7,6},{8,9},{9,8},{10,11... | collective-permute-start | bytes 3145736 | tf_op jit(solution)/shard_map/ppermute | solution.py:136
  35.9 1.9 %collective-permute-start.5 = (bf16[256,2048]{1,0:T(8,128)(2,1)}, bf16[256,2048]{1,0:T(8,128)(2,1)}, u32[]{:S(2)}, u32[]{:S(2)}) collective-permute-start(bf16[256,2048]{1,0:T(8,128)(2,1)} %get-tuple-element.11), channel_id=1, source_target_pairs={{0,1},{1,0},{2,3},{3,2},{4,5},{5,4},{6,7},{7,6},{8,9},{9,8},{10,11... | collective-permute-start | bytes 3145736 | tf_op jit(solution)/shard_map/ppermute | solution.py:136
  37.9 2.4 %collective-permute-start.6 = (bf16[256,2048]{1,0:T(8,128)(2,1)}, bf16[256,2048]{1,0:T(8,128)(2,1)}, u32[]{:S(2)}, u32[]{:S(2)}) collective-permute-start(bf16[256,2048]{1,0:T(8,128)(2,1)} %get-tuple-element.12), channel_id=1, source_target_pairs={{0,1},{1,0},{2,3},{3,2},{4,5},{5,4},{6,7},{7,6},{8,9},{9,8},{10,11... | collective-permute-start | bytes 3145736 | tf_op jit(solution)/shard_map/ppermute | solution.py:136
  40.3 0.0 copy-start.6
  40.3 0.0 copy-start.8
  40.3 0.0 collective-permute-done.2
  40.3 3.6 %collective-permute-start.3 = (bf16[2,128,2048]{2,1,0:T(8,128)(2,1)}, bf16[2,128,2048]{2,1,0:T(8,128)(2,1)S(1)}, u32[]{:S(2)}, u32[]{:S(2)}) collective-permute-start(bf16[2,128,2048]{2,1,0:T(8,128)(2,1)} %collective-permute-done.2), channel_id=1, source_target_pairs={{1,65},{3,67},{5,69},{7,71},{9,73},{11,75},{13,77},{15,79},{17,81}... | collective-permute-start | bytes 3145736 | tf_op jit(solution)/shard_map/ppermute | solution.py:140
  44.0 0.0 collective-permute-done.1
  44.0 4.3 %collective-permute-start.7 = (bf16[2,128,2048]{2,1,0:T(8,128)(2,1)}, bf16[2,128,2048]{2,1,0:T(8,128)(2,1)S(1)}, u32[]{:S(2)}, u32[]{:S(2)}) collective-permute-start(bf16[2,128,2048]{2,1,0:T(8,128)(2,1)} %collective-permute-done.1), channel_id=1, source_target_pairs={{1,449},{3,451},{5,453},{7,455},{9,457},{11,459},{13,461},{15,463}... | collective-permute-start | bytes 3145736 | tf_op jit(solution)/shard_map/ppermute | solution.py:141
  48.3 0.0 collective-permute-done.4
  48.3 1.3 %constant_dynamic-update-slice_fusion.2 = bf16[768,2048]{1,0:T(8,128)(2,1)S(1)} fusion(bf16[256,2048]{1,0:T(8,128)(2,1)} %collective-permute-done.4), kind=kLoop, calls=%fused_computation.34 | loop fusion | bytes 2097152
  49.6 0.0 collective-permute-done.5
  49.6 1.3 %constant_dynamic-update-slice_fusion.1 = bf16[768,2048]{1,0:T(8,128)(2,1)S(1)} fusion(bf16[768,2048]{1,0:T(8,128)(2,1)S(1)} %constant_dynamic-update-slice_fusion.2, bf16[256,2048]{1,0:T(8,128)(2,1)} %collective-permute-done.5), kind=kLoop, calls=%fused_computation.33 | loop fusion | bytes 2097152
  50.9 0.0 collective-permute-done.6
  50.9 1.3 %constant_dynamic-update-slice_fusion = bf16[768,2048]{1,0:T(8,128)(2,1)S(1)} fusion(bf16[768,2048]{1,0:T(8,128)(2,1)S(1)} %constant_dynamic-update-slice_fusion.1, bf16[256,2048]{1,0:T(8,128)(2,1)} %collective-permute-done.6), kind=kLoop, calls=%fused_computation.32 | loop fusion | bytes 2097152 | tf_op jit(solution)/shard_map/concatenate | solution.py:135
  52.2 0.0 copy-done.6
  52.2 0.0 copy-done.8
  52.2 1.4 %broadcast_select_fusion.2 = bf16[2,128,2048]{2,1,0:T(8,128)(2,1)S(1)} fusion(bf16[2,128,2048]{2,1,0:T(8,128)(2,1)} %collective-permute-done.1, pred[]{:T(512)S(6)} %eq.3, bf16[1,128,2048]{2,1,0:T(8,128)(2,1)S(1)} %bitcast.42, bf16[1,128,2048]{2,1,0:T(8,128)(2,1)S(1)} %bitcast.39), kind=kLoop, calls=%fused_computation.26 | loop fusion | flops 1048576 | bytes 3145729 | tf_op jit(solution)/shard_map/jit(_where)/select_n | solution.py:150
  53.6 2.9 %collective-permute-done.3 = bf16[2,128,2048]{2,1,0:T(8,128)(2,1)S(1)} collective-permute-done((bf16[2,128,2048]{2,1,0:T(8,128)(2,1)}, bf16[2,128,2048]{2,1,0:T(8,128)(2,1)S(1)}, u32[]{:S(2)}, u32[]{:S(2)}) %collective-permute-start.3) | collective-permute-done | bytes 1048608 | tf_op jit(solution)/shard_map/ppermute | solution.py:140
  56.5 1.3 %collective-permute-start.9 = (bf16[2,128,2048]{2,1,0:T(8,128)(2,1)S(1)}, bf16[2,128,2048]{2,1,0:T(8,128)(2,1)S(1)}, u32[]{:S(2)}, u32[]{:S(2)}) collective-permute-start(bf16[2,128,2048]{2,1,0:T(8,128)(2,1)S(1)} %collective-permute-done.3), channel_id=1, source_target_pairs={{0,64},{2,66},{4,68},{6,70},{8,72},{10,74},{12,76},{14,78},{16,80}... | collective-permute-start | bytes 3145736 | tf_op jit(solution)/shard_map/ppermute | solution.py:140
  57.8 3.0 %collective-permute-done.7 = bf16[2,128,2048]{2,1,0:T(8,128)(2,1)S(1)} collective-permute-done((bf16[2,128,2048]{2,1,0:T(8,128)(2,1)}, bf16[2,128,2048]{2,1,0:T(8,128)(2,1)S(1)}, u32[]{:S(2)}, u32[]{:S(2)}) %collective-permute-start.7) | collective-permute-done | bytes 1048608 | tf_op jit(solution)/shard_map/ppermute | solution.py:141
  60.8 1.3 %collective-permute-start.8 = (bf16[2,128,2048]{2,1,0:T(8,128)(2,1)S(1)}, bf16[2,128,2048]{2,1,0:T(8,128)(2,1)S(1)}, u32[]{:S(2)}, u32[]{:S(2)}) collective-permute-start(bf16[2,128,2048]{2,1,0:T(8,128)(2,1)S(1)} %collective-permute-done.7), channel_id=1, source_target_pairs={{0,448},{2,450},{4,452},{6,454},{8,456},{10,458},{12,460},{14,462}... | collective-permute-start | bytes 3145736 | tf_op jit(solution)/shard_map/ppermute | solution.py:141
  62.1 1.3 %broadcast_select_fusion.1 = bf16[2,128,2048]{2,1,0:T(8,128)(2,1)S(1)} fusion(bf16[2,128,2048]{2,1,0:T(8,128)(2,1)S(1)} %collective-permute-done.3, bf16[2,128,2048]{2,1,0:T(8,128)(2,1)} %collective-permute-done.2, pred[]{:T(512)S(6)} %eq.3), kind=kLoop, calls=%fused_computation.25 | loop fusion | flops 524288 | bytes 3145729 | tf_op jit(solution)/shard_map/jit(_where)/select_n | solution.py:153
  63.4 1.0 fusion.25
  64.5 1.1 fusion.17
  65.6 11.5 %collective-permute-done.9 = bf16[2,128,2048]{2,1,0:T(8,128)(2,1)S(1)} collective-permute-done((bf16[2,128,2048]{2,1,0:T(8,128)(2,1)S(1)}, bf16[2,128,2048]{2,1,0:T(8,128)(2,1)S(1)}, u32[]{:S(2)}, u32[]{:S(2)}) %collective-permute-start.9) | collective-permute-done | bytes 1048608 | tf_op jit(solution)/shard_map/ppermute | solution.py:140
  77.2 1.3 %collective-permute-start.10 = (bf16[2,64,2048]{2,1,0:T(8,128)(2,1)S(1)}, bf16[2,64,2048]{2,1,0:T(8,128)(2,1)S(1)}, u32[]{:S(2)}, u32[]{:S(2)}) collective-permute-start(bf16[2,64,2048]{2,1,0:T(8,128)(2,1)S(1)} %slice.48), channel_id=1, source_target_pairs={{1,65},{3,67},{5,69},{7,71},{9,73},{11,75},{13,77},{15,79},{17,81}... | collective-permute-start | bytes 1572872 | tf_op jit(solution)/shard_map/ppermute | solution.py:144
  78.5 0.0 collective-permute-done.8
  78.6 1.7 %collective-permute-start.11 = (bf16[2,64,2048]{2,1,0:T(8,128)(2,1)S(1)}, bf16[2,64,2048]{2,1,0:T(8,128)(2,1)S(1)}, u32[]{:S(2)}, u32[]{:S(2)}) collective-permute-start(bf16[2,64,2048]{2,1,0:T(8,128)(2,1)S(1)} %slice.49), channel_id=1, source_target_pairs={{1,449},{3,451},{5,453},{7,455},{9,457},{11,459},{13,461},{15,463}... | collective-permute-start | bytes 1572872 | tf_op jit(solution)/shard_map/ppermute | solution.py:145
  80.3 0.1 broadcast_select_fusion
  80.4 4.7 %collective-permute-done.10 = bf16[2,64,2048]{2,1,0:T(8,128)(2,1)S(1)} collective-permute-done((bf16[2,64,2048]{2,1,0:T(8,128)(2,1)S(1)}, bf16[2,64,2048]{2,1,0:T(8,128)(2,1)S(1)}, u32[]{:S(2)}, u32[]{:S(2)}) %collective-permute-start.10) | collective-permute-done | bytes 524320 | tf_op jit(solution)/shard_map/ppermute | solution.py:144
  85.2 1.8 %collective-permute-done.11 = bf16[2,64,2048]{2,1,0:T(8,128)(2,1)S(1)} collective-permute-done((bf16[2,64,2048]{2,1,0:T(8,128)(2,1)S(1)}, bf16[2,64,2048]{2,1,0:T(8,128)(2,1)S(1)}, u32[]{:S(2)}, u32[]{:S(2)}) %collective-permute-start.11) | collective-permute-done | bytes 524320 | tf_op jit(solution)/shard_map/ppermute | solution.py:145
  87.0 0.4 maximum_select_fusion
  87.3 1.0 fusion.21
  88.4 1.1 fusion.7
  89.5 0.1 slice_bitcast_fusion.2
  89.6 0.1 pad_maximum_fusion.3
  89.7 26.9 %all_to_all.11 = bf16[4,128,768]{2,1,0:T(8,128)(2,1)S(1)} all-to-all(bf16[4,128,768]{2,1,0:T(8,128)(2,1)S(1)} %pad_maximum_fusion.3), channel_id=1, replica_groups={{0,2,4,6},{1,3,5,7},{8,10,12,14},{9,11,13,15},{16,18,20,22},{17,19,21,2..., dimensions={0} | all-to-all | bytes 1572864 | tf_op jit(solution)/shard_map/all_to_all | solution.py:160
  116.6 0.8 reduce_sum.12
  (5 shorter events, 0.1 us)
Async XLA Ops:
  0.0 23.0 %copy-start.9 = (f32[768]{0:T(1024)S(1)}, f32[768]{0:T(1024)}, u32[]{:S(2)}) copy-start(f32[768]{0:T(1024)} %param.11) | copy-start | bytes 9220
  0.0 23.1 %copy-start.3 = (bf16[16,2048]{1,0:T(8,128)(2,1)S(1)}, bf16[16,2048]{1,0:T(8,128)(2,1)}, u32[]{:S(2)}) copy-start(bf16[16,2048]{1,0:T(8,128)(2,1)} %up_ref.1) | copy-start | bytes 196612
  0.0 23.1 %copy-start.4 = (bf16[768,16]{0,1:T(8,128)(2,1)S(1)}, bf16[768,16]{0,1:T(8,128)(2,1)}, u32[]{:S(2)}) copy-start(bf16[768,16]{0,1:T(8,128)(2,1)} %param.12) | copy-start | bytes 73732
  0.0 23.1 %copy-start.2 = (f32[6,2048]{1,0:T(8,128)S(1)}, f32[6,2048]{1,0:T(8,128)}, u32[]{:S(2)}) copy-start(f32[6,2048]{1,0:T(8,128)} %scale_ref.1) | copy-start | bytes 147460
  0.0 23.1 %copy-start.1 = (s32[6,2048]{1,0:T(8,128)S(1)}, s32[6,2048]{1,0:T(8,128)}, u32[]{:S(2)}) copy-start(s32[6,2048]{1,0:T(8,128)} %zero_ref.1) | copy-start | bytes 147460
  0.0 23.1 %copy-start = (s32[768,1024]{1,0:T(8,128)S(1)}, s32[768,1024]{1,0:T(8,128)}, u32[]{:S(2)}) copy-start(s32[768,1024]{1,0:T(8,128)} %words_ref.1) | copy-start | bytes 9437188
  16.4 11.8 %copy-start.5 = (bf16[8,16,2048]{2,1,0:T(8,128)(2,1)}, bf16[8,16,2048]{2,1,0:T(8,128)(2,1)S(1)}, u32[]{:S(2)}) copy-start(bf16[8,16,2048]{2,1,0:T(8,128)(2,1)S(1)} %all_to_all.10) | copy-start | bytes 1572868
  16.4 2.8 %collective-permute-start = (bf16[128,2048]{1,0:T(8,128)(2,1)S(1)}, bf16[128,2048]{1,0:T(8,128)(2,1)S(1)}, u32[]{:S(2)}, u32[]{:S(2)}) collective-permute-start(bf16[128,2048]{1,0:T(8,128)(2,1)S(1)} %bitcast.37), channel_id=1, source_target_pairs={{1,0},{3,2},{5,4},{7,6},{9,8},{11,10},{13,12},{15,14},{17,16},{19,... | collective-permute-start | bytes 1572872 | tf_op jit(solution)/shard_map/ppermute | solution.py:132
  19.3 9.0 %copy-start.7 = (bf16[128,2048]{1,0:T(8,128)(2,1)}, bf16[128,2048]{1,0:T(8,128)(2,1)S(1)}, u32[]{:S(2)}) copy-start(bf16[128,2048]{1,0:T(8,128)(2,1)S(1)} %collective-permute-done) | copy-start | bytes 1572868
  20.4 19.9 %collective-permute-start.2 = (bf16[2,128,2048]{2,1,0:T(8,128)(2,1)}, bf16[2,128,2048]{2,1,0:T(8,128)(2,1)}, u32[]{:S(2)}, u32[]{:S(2)}) collective-permute-start(bf16[2,128,2048]{2,1,0:T(8,128)(2,1)} %pad_maximum_fusion.2), channel_id=1, source_target_pairs={{0,64},{2,66},{4,68},{6,70},{8,72},{10,74},{12,76},{14,78},{16,80}... | collective-permute-start | bytes 3145736 | tf_op jit(solution)/shard_map/ppermute | solution.py:140
  21.7 22.3 %collective-permute-start.1 = (bf16[2,128,2048]{2,1,0:T(8,128)(2,1)}, bf16[2,128,2048]{2,1,0:T(8,128)(2,1)}, u32[]{:S(2)}, u32[]{:S(2)}) collective-permute-start(bf16[2,128,2048]{2,1,0:T(8,128)(2,1)} %pad_maximum_fusion.2), channel_id=1, source_target_pairs={{0,448},{2,450},{4,452},{6,454},{8,456},{10,458},{12,460},{14,462}... | collective-permute-start | bytes 3145736 | tf_op jit(solution)/shard_map/ppermute | solution.py:141
  28.3 20.0 %collective-permute-start.4 = (bf16[256,2048]{1,0:T(8,128)(2,1)}, bf16[256,2048]{1,0:T(8,128)(2,1)}, u32[]{:S(2)}, u32[]{:S(2)}) collective-permute-start(bf16[256,2048]{1,0:T(8,128)(2,1)} %get-tuple-element.10), channel_id=1, source_target_pairs={{0,1},{1,0},{2,3},{3,2},{4,5},{5,4},{6,7},{7,6},{8,9},{9,8},{10,11... | collective-permute-start | bytes 3145736 | tf_op jit(solution)/shard_map/ppermute | solution.py:136
  35.9 13.6 %collective-permute-start.5 = (bf16[256,2048]{1,0:T(8,128)(2,1)}, bf16[256,2048]{1,0:T(8,128)(2,1)}, u32[]{:S(2)}, u32[]{:S(2)}) collective-permute-start(bf16[256,2048]{1,0:T(8,128)(2,1)} %get-tuple-element.11), channel_id=1, source_target_pairs={{0,1},{1,0},{2,3},{3,2},{4,5},{5,4},{6,7},{7,6},{8,9},{9,8},{10,11... | collective-permute-start | bytes 3145736 | tf_op jit(solution)/shard_map/ppermute | solution.py:136
  37.9 13.0 %collective-permute-start.6 = (bf16[256,2048]{1,0:T(8,128)(2,1)}, bf16[256,2048]{1,0:T(8,128)(2,1)}, u32[]{:S(2)}, u32[]{:S(2)}) collective-permute-start(bf16[256,2048]{1,0:T(8,128)(2,1)} %get-tuple-element.12), channel_id=1, source_target_pairs={{0,1},{1,0},{2,3},{3,2},{4,5},{5,4},{6,7},{7,6},{8,9},{9,8},{10,11... | collective-permute-start | bytes 3145736 | tf_op jit(solution)/shard_map/ppermute | solution.py:136
  40.3 11.9 %copy-start.6 = (bf16[8,16,2048]{2,1,0:T(8,128)(2,1)S(1)}, bf16[8,16,2048]{2,1,0:T(8,128)(2,1)}, u32[]{:S(2)}) copy-start(bf16[8,16,2048]{2,1,0:T(8,128)(2,1)} %copy-done.5) | copy-start | bytes 1572868
  40.3 11.9 %copy-start.8 = (bf16[128,2048]{1,0:T(8,128)(2,1)S(1)}, bf16[128,2048]{1,0:T(8,128)(2,1)}, u32[]{:S(2)}) copy-start(bf16[128,2048]{1,0:T(8,128)(2,1)} %copy-done.7) | copy-start | bytes 1572868
  40.3 16.2 %collective-permute-start.3 = (bf16[2,128,2048]{2,1,0:T(8,128)(2,1)}, bf16[2,128,2048]{2,1,0:T(8,128)(2,1)S(1)}, u32[]{:S(2)}, u32[]{:S(2)}) collective-permute-start(bf16[2,128,2048]{2,1,0:T(8,128)(2,1)} %collective-permute-done.2), channel_id=1, source_target_pairs={{1,65},{3,67},{5,69},{7,71},{9,73},{11,75},{13,77},{15,79},{17,81}... | collective-permute-start | bytes 3145736 | tf_op jit(solution)/shard_map/ppermute | solution.py:140
  44.0 16.8 %collective-permute-start.7 = (bf16[2,128,2048]{2,1,0:T(8,128)(2,1)}, bf16[2,128,2048]{2,1,0:T(8,128)(2,1)S(1)}, u32[]{:S(2)}, u32[]{:S(2)}) collective-permute-start(bf16[2,128,2048]{2,1,0:T(8,128)(2,1)} %collective-permute-done.1), channel_id=1, source_target_pairs={{1,449},{3,451},{5,453},{7,455},{9,457},{11,459},{13,461},{15,463}... | collective-permute-start | bytes 3145736 | tf_op jit(solution)/shard_map/ppermute | solution.py:141
  56.5 20.6 %collective-permute-start.9 = (bf16[2,128,2048]{2,1,0:T(8,128)(2,1)S(1)}, bf16[2,128,2048]{2,1,0:T(8,128)(2,1)S(1)}, u32[]{:S(2)}, u32[]{:S(2)}) collective-permute-start(bf16[2,128,2048]{2,1,0:T(8,128)(2,1)S(1)} %collective-permute-done.3), channel_id=1, source_target_pairs={{0,64},{2,66},{4,68},{6,70},{8,72},{10,74},{12,76},{14,78},{16,80}... | collective-permute-start | bytes 3145736 | tf_op jit(solution)/shard_map/ppermute | solution.py:140
  60.8 17.7 %collective-permute-start.8 = (bf16[2,128,2048]{2,1,0:T(8,128)(2,1)S(1)}, bf16[2,128,2048]{2,1,0:T(8,128)(2,1)S(1)}, u32[]{:S(2)}, u32[]{:S(2)}) collective-permute-start(bf16[2,128,2048]{2,1,0:T(8,128)(2,1)S(1)} %collective-permute-done.7), channel_id=1, source_target_pairs={{0,448},{2,450},{4,452},{6,454},{8,456},{10,458},{12,460},{14,462}... | collective-permute-start | bytes 3145736 | tf_op jit(solution)/shard_map/ppermute | solution.py:141
  77.2 8.0 %collective-permute-start.10 = (bf16[2,64,2048]{2,1,0:T(8,128)(2,1)S(1)}, bf16[2,64,2048]{2,1,0:T(8,128)(2,1)S(1)}, u32[]{:S(2)}, u32[]{:S(2)}) collective-permute-start(bf16[2,64,2048]{2,1,0:T(8,128)(2,1)S(1)} %slice.48), channel_id=1, source_target_pairs={{1,65},{3,67},{5,69},{7,71},{9,73},{11,75},{13,77},{15,79},{17,81}... | collective-permute-start | bytes 1572872 | tf_op jit(solution)/shard_map/ppermute | solution.py:144
  78.6 8.4 %collective-permute-start.11 = (bf16[2,64,2048]{2,1,0:T(8,128)(2,1)S(1)}, bf16[2,64,2048]{2,1,0:T(8,128)(2,1)S(1)}, u32[]{:S(2)}, u32[]{:S(2)}) collective-permute-start(bf16[2,64,2048]{2,1,0:T(8,128)(2,1)S(1)} %slice.49), channel_id=1, source_target_pairs={{1,449},{3,451},{5,453},{7,455},{9,457},{11,459},{13,461},{15,463}... | collective-permute-start | bytes 1572872 | tf_op jit(solution)/shard_map/ppermute | solution.py:145
